TPU v7x, 512 devices: a whole 4x4x16 slice. The times are simulated.
512 devices in a mesh: kb: 32 (over z, core), gr: 4 (over y), gc: 4 (over x).
Axes of the slice: x: 4, y: 4, z: 16, core: 2. Of those that a mesh axis runs over, the one named last changes fastest.
Arguments:
- wedge_pairs: bfloat16 [32, 1, 16, 2048], P('kb'), may hold values from -6 to 6
- e_cond: float32 [32, 1], P('kb'), may hold values from 0.5 to 12
- e_val: float32 [32, 16], P('kb'), may hold values from -8 to -1
- coulomb: float32 [2048], replicated, may hold values from 0.5 to 50
- owned_wedge: int32 [32, 17], replicated, may hold values from -1 to 31, as said below
- owned_op: int32 [32, 17], replicated, may hold values from 0 to 47
- gmap: int32 [48, 2048], replicated, may hold values from 0 to 2047, each once within a row
Outputs:
- panel_step: float32 [2048, 2048], P(('gr', 'kb'), 'gc')
Inputs may be any that keep to these rules, and one draw needn't show every extreme that they name: `owned_wedge`: each owner lists 16 or 17 wedge k points in its first slots, the rest -1; no owner lists a wedge twice; some owner lists exactly 17. `gmap`: each row is a permutation of the plane waves.
All inputs are finite; a program needn't handle non-finite values.
Results may differ from a plain program's by a relative error of at most 0.0024.
Values may be sent and summed in bfloat16 or wider, within the bound.
A program may use at most 64 MiB of HBM per device.

v0:
```python
import jax
import jax.numpy as jnp
from jax import lax
from jax.sharding import PartitionSpec as P


def broadcast(block, axis, holder):
    block = jnp.where(lax.axis_index(axis) == holder, block, jnp.zeros_like(block))
    return lax.psum(block, axis)


def body(wedge_pairs, e_cond, e_val, coulomb, owned_wedge, owned_op, gmap):
    groups = lax.axis_size("kb")
    grid = lax.axis_size("gr")
    total_g = gmap.shape[1]
    width = total_g // grid
    band_rows = width // groups
    slot_count = owned_wedge.shape[1]
    row_block = lax.axis_index("gr")
    col_block = lax.axis_index("gc")
    member = lax.axis_index("kb")
    columns = jnp.concatenate(
        [
            row_block * width + jnp.arange(width, dtype=jnp.int32),
            col_block * width + jnp.arange(width, dtype=jnp.int32),
        ]
    )
    matched = owned_wedge == member
    present = jnp.any(matched, axis=1).astype(jnp.float32)
    operation = jnp.sum(jnp.where(matched, owned_op, 0), axis=1)
    taken = gmap[operation[:, None], columns[None, :]]
    own_rows = wedge_pairs[0].reshape(-1, total_g)
    slot_gap = e_cond[0][:, None] - e_val[0][None, :]
    kpoint_weight = jnp.sqrt(4.0 / (float(groups * slot_count) * slot_gap)).reshape(-1)
    picked = jnp.take(own_rows, taken, axis=1)
    outgoing = (
        picked.astype(jnp.float32) * kpoint_weight[:, None, None] * present[None, :, None]
    ).astype(jnp.bfloat16)
    arrived = lax.all_to_all(outgoing, "kb", split_axis=1, concat_axis=1, tiled=True)
    mine = owned_wedge[member]
    valid_mask = mine >= 0
    chosen = arrived[:, jnp.maximum(mine, 0), :]
    chosen = jnp.where(valid_mask[None, :, None], chosen, jnp.zeros((), jnp.bfloat16))
    pairs = chosen.reshape(-1, 2 * width)
    left = lax.slice_in_dim(pairs, 0, band_rows * lax.axis_size("kb"), axis=1)
    right = pairs[:, width:]
    chi_rows = lax.psum_scatter(
        -lax.dot_general(left, right, (((0,), (0,)), ((), ())), preferred_element_type=jnp.float32),
        "kb",
        scatter_dimension=0,
        tiled=True,
    )
    row_ids = row_block * width + member * band_rows + jnp.arange(band_rows, dtype=jnp.int32)
    col_ids = col_block * width + jnp.arange(width, dtype=jnp.int32)
    root = jnp.sqrt(coulomb)
    identity = (row_ids[:, None] == col_ids[None, :]).astype(jnp.float32)
    eps_rows = identity - root[row_ids][:, None] * chi_rows * root[col_ids][None, :]
    gathered = lax.all_gather(eps_rows, "kb", axis=0, tiled=True)
    top = broadcast(gathered, "gr", 0)
    diagonal, left_rows = (broadcast(top, "gc", 0), broadcast(eps_rows, "gc", 0))
    factor = jnp.linalg.cholesky(diagonal)
    lower_rows = lax.linalg.triangular_solve(
        factor, left_rows, left_side=False, lower=True, transpose_a=True
    )
    upper_block = lax.linalg.triangular_solve(factor, top, left_side=True, lower=True)
    trail = eps_rows - jnp.dot(lower_rows, upper_block, precision=lax.Precision.HIGHEST)
    factor_rows = lax.dynamic_slice_in_dim(factor, member * band_rows, band_rows, 0)
    first_col = jnp.where(row_block == 0, factor_rows, lower_rows)
    other_col = jnp.where(row_block == 0, eps_rows, trail)
    return jnp.where(col_block == 0, first_col, other_col)


def solution(mesh):
    placed = (P("kb", None, None, None), P("kb", None), P("kb", None), P(), P(), P(), P())
    return jax.shard_map(
        body, mesh=mesh, in_specs=placed, out_specs=P(("gr", "kb"), "gc"), check_vma=False
    )
```

profile of v0, /device:TPU:1, one launch (start us, length us, event | category | flops | bytes accessed | tf_op | source)
XLA Modules:
  0.0 922.7 jit_solution(10629733440315858376)
XLA Ops:
  7.6 258.4 %gather_fusion.1 = s32[32768]{0:T(1024)S(1)} fusion(s32[48,2048]{1,0:T(8,128)S(1)} %copy-done, s32[32768]{0:T(1024)S(1)} %bitcast.75), kind=kCustom, calls=%fused_computation.1 | custom fusion | bytes 524288 | tf_op jit(solution)/shard_map/gather | solution.py:31
  266.4 114.2 %gather_fusion.2 = bf16[32768,16]{1,0:T(8,128)(2,1)} fusion(bf16[16,2048]{0,1:T(8,128)(2,1)S(1)} %bitcast.76, s32[32768]{0:T(1024)S(1)} %broadcast_clamp_fusion), kind=kCustom, calls=%fused_computation.2 | custom fusion | bytes 2228224 | tf_op jit(solution)/shard_map/jit(_take)/gather | solution.py:35
  380.6 6.7 copy.68
  388.1 1.4 fusion.2
  389.5 16.8 %all-to-all-start = ((bf16[16,32,1024]{2,0,1:T(8,128)(2,1)}), bf16[16,32,1024]{2,0,1:T(8,128)(2,1)S(1)}, u32[]{:S(2)}, u32[]{:S(2)}) async-start(bf16[16,32,1024]{2,0,1:T(8,128)(2,1)} %fusion.2), calls=%async_computation | async-start | bytes 2097152 | tf_op jit(solution)/shard_map/all_to_all | solution.py:39
  406.8 55.2 %all-to-all-done = bf16[16,32,1024]{2,0,1:T(8,128)(2,1)S(1)} async-done(((bf16[16,32,1024]{2,0,1:T(8,128)(2,1)}), bf16[16,32,1024]{2,0,1:T(8,128)(2,1)S(1)}, u32[]{:S(2)}, u32[]{:S(2)}) %all-to-all-start) | async-done | bytes 1048608 | tf_op jit(solution)/shard_map/all_to_all | solution.py:39
  463.3 1.5 convolution_negate_fusion
  465.5 3.1 gather_fusion.4
  468.7 93.1 %reduce-scatter.4.cloned.1.call-done = f32[16,512]{1,0:T(8,128)} async-done(((f32[512,512]{1,0:T(8,128)}), f32[16,512]{1,0:T(8,128)}) %reduce-scatter.4.cloned.1.call-update) | async-done | bytes 32784
  563.7 72.2 %all-gather.2.cloned.1.call-done = f32[512,512]{1,0:T(8,128)} async-done(((f32[16,512]{1,0:T(8,128)}), f32[512,512]{1,0:T(8,128)}) %all-gather.2.cloned.1.call-update) | async-done | bytes 1048592 | tf_op jit(solution)/shard_map/all_gather | solution.py:58
  635.9 1.6 copy.72
  638.6 56.7 %all-reduce.4.cloned.1.call-done = f32[512,512]{0,1:T(8,128)} async-done(((f32[512,512]{0,1:T(8,128)}), f32[512,512]{0,1:T(8,128)}) %all-reduce.4.cloned.1.call-update) | async-done | bytes 1048592 | tf_op jit(solution)/shard_map/psum | solution.py:9
  695.3 2.3 broadcast_select_fusion.1
  697.7 16.2 %psum.23 = f32[16,512]{0,1:T(8,128)} all-reduce(f32[16,512]{0,1:T(8,128)S(1)} %get-tuple-element.37), channel_id=1, replica_groups=mesh['kb'=32,'gr'=4,'gc'=4] {'gc'}, use_global_device_ids=true, to_apply=%region_13.14 | all-reduce | flops 8192 | bytes 65536 | tf_op jit(solution)/shard_map/psum | solution.py:9
  713.9 45.9 %all-reduce.6.cloned.1.call-done = f32[512,512]{0,1:T(8,128)} async-done(((f32[512,512]{0,1:T(8,128)}), f32[512,512]{0,1:T(8,128)}) %all-reduce.6.cloned.1.call-update) | async-done | bytes 1048592 | tf_op jit(solution)/shard_map/psum | solution.py:9
  759.8 1.6 copy.73
  761.3 1.5 fusion.10
  762.9 11.7 %cholesky.103 = f32[128,128]{1,0:T(8,128)S(1)} custom-call(f32[128,128]{1,0:T(8,128)S(1)} %cholesky.263), custom_call_target="Cholesky" | custom-call | tf_op jit(solution)/shard_map/jit(cholesky)/cholesky | solution.py:61
  774.6 9.8 %custom-call.32 = f32[1,128,128]{1,2,0:T(8,128)S(1)} custom-call(f32[1,128,128]{2,1,0:T(8,128)S(1)} %get-tuple-element.50), custom_call_target="InvertDiagBlocksLowerTriangular" | custom-call | tf_op jit(solution)/shard_map/jit(cholesky)/cholesky | solution.py:61
  785.1 11.7 %cholesky.215 = f32[128,128]{1,0:T(8,128)S(1)} custom-call(f32[128,128]{1,0:T(8,128)S(1)} %cholesky.267), custom_call_target="Cholesky" | custom-call | tf_op jit(solution)/shard_map/jit(cholesky)/cholesky | solution.py:61
  797.2 10.0 %custom-call.33 = f32[1,128,128]{1,2,0:T(8,128)S(1)} custom-call(f32[1,128,128]{2,1,0:T(8,128)S(1)} %get-tuple-element.48), custom_call_target="InvertDiagBlocksLowerTriangular" | custom-call | tf_op jit(solution)/shard_map/jit(cholesky)/cholesky | solution.py:61
  807.7 1.5 convolution_subtract_fusion.5
  809.2 11.7 %cholesky.236 = f32[128,128]{1,0:T(8,128)S(1)} custom-call(f32[128,128]{1,0:T(8,128)S(1)} %cholesky.272), custom_call_target="Cholesky" | custom-call | tf_op jit(solution)/shard_map/jit(cholesky)/cholesky | solution.py:61
  821.0 9.8 %custom-call.34 = f32[1,128,128]{1,2,0:T(8,128)S(1)} custom-call(f32[1,128,128]{2,1,0:T(8,128)S(1)} %get-tuple-element.46), custom_call_target="InvertDiagBlocksLowerTriangular" | custom-call | tf_op jit(solution)/shard_map/jit(cholesky)/cholesky | solution.py:61
  832.5 11.9 %cholesky.253 = f32[128,128]{1,0:T(8,128)S(1)} custom-call(f32[128,128]{1,0:T(8,128)S(1)} %convolution_subtract_fusion.9), custom_call_target="Cholesky" | custom-call | tf_op jit(solution)/shard_map/jit(cholesky)/cholesky | solution.py:61
  851.0 10.7 %while.1 = (s32[]{:T(128)}, f32[512,512]{0,1:T(8,128)S(1)}, s32[4,2]{0,1:T(2,128)S(1)}, f32[4,128,128]{2,1,0:T(8,128)}, s32[]{:T(128)}) while((s32[]{:T(128)}, f32[512,512]{0,1:T(8,128)S(1)}, s32[4,2]{0,1:T(2,128)S(1)}, f32[4,128,128]{2,1,0:T(8,128)}, s32[]{:T(128)}) %tuple.30), condition=%wide.while_cond, body=%wide.while_body.sunk | while | flops 2 | bytes 393829 | solution.py:62
  851.6 1.4 dynamic-slice.7
  854.3 1.4 dynamic-slice.7
  861.7 40.1 %custom-call.35 = f32[4,128,128]{1,2,0:T(8,128)S(1)} custom-call(f32[4,128,128]{2,1,0:T(8,128)} %get-tuple-element.12), custom_call_target="InvertDiagBlocksLowerTriangular" | custom-call | tf_op jit(solution)/shard_map/triangular_solve | solution.py:62
  905.8 1.4 convolution_subtract_fusion.6
  910.5 1.5 convolution_subtract_fusion.2
  912.3 2.8 fusion.1
  (123 shorter events, 30.7 us)
Async XLA Ops:
  6.5 1.0 copy-start
  7.6 258.6 %copy-start.5 = (bf16[1,1,16,2048]{3,2,1,0:T(8,128)(2,1)S(1)}, bf16[1,1,16,2048]{3,2,1,0:T(8,128)(2,1)}, u32[]{:S(2)}) copy-start(bf16[1,1,16,2048]{3,2,1,0:T(8,128)(2,1)} %param.7) | copy-start | bytes 196612
  266.4 121.7 %copy-start.7 = (f32[1,16]{1,0:T(1,128)S(1)}, f32[1,16]{1,0:T(1,128)}, u32[]{:S(2)}) copy-start(f32[1,16]{1,0:T(1,128)} %param.9) | copy-start | bytes 196
  380.6 25.7 %copy-start.4 = (s32[32,17]{0,1:T(8,128)S(1)}, s32[32,17]{0,1:T(8,128)}, u32[]{:S(2)}) copy-start(s32[32,17]{0,1:T(8,128)} %param.11) | copy-start | bytes 6532
  387.4 77.4 %copy-start.6 = (f32[2048]{0:T(1024)S(1)}, f32[2048]{0:T(1024)}, u32[]{:S(2)}) copy-start(f32[2048]{0:T(1024)} %param.10) | copy-start | bytes 24580
  389.5 72.5 %all-to-all-start = ((bf16[16,32,1024]{2,0,1:T(8,128)(2,1)}), bf16[16,32,1024]{2,0,1:T(8,128)(2,1)S(1)}, u32[]{:S(2)}, u32[]{:S(2)}) async-start(bf16[16,32,1024]{2,0,1:T(8,128)(2,1)} %fusion.2), calls=%async_computation | async-start | bytes 2097152 | tf_op jit(solution)/shard_map/all_to_all | solution.py:39
  406.3 155.5 %reduce-scatter.4.cloned.1.call-start = ((), (), s32[]{:S(2)}) async-start(), calls=%async_computation.5 | async-start | bytes 1081344
  464.7 171.1 %all-gather.2.cloned.1.call-start = ((), (), s32[]{:S(2)}) async-start(), calls=%async_computation.2 | async-start | bytes 1081344 | tf_op jit(solution)/shard_map/all_gather | solution.py:58
  562.9 0.8 copy-start.3
  563.7 131.7 %all-reduce.4.cloned.1.call-start = ((), (), s32[]{:S(2)}) async-start(), calls=%async_computation.3 | async-start | bytes 2097152 | tf_op jit(solution)/shard_map/psum | solution.py:9
  638.6 121.2 %all-reduce.6.cloned.1.call-start = ((), (), s32[]{:S(2)}) async-start(), calls=%async_computation.4 | async-start | bytes 2097152 | tf_op jit(solution)/shard_map/psum | solution.py:9
  761.3 146.2 %copy-start.1 = (f32[512,512]{0,1:T(8,128)S(1)}, f32[512,512]{0,1:T(8,128)}, u32[]{:S(2)}) copy-start(f32[512,512]{0,1:T(8,128)} %all-reduce.4.cloned.1.call-done) | copy-start | bytes 3145732
  762.9 34.3 %copy-start.2 = (f32[512,512]{1,0:T(8,128)}, f32[512,512]{1,0:T(8,128)S(1)}, u32[]{:S(2)}) copy-start(f32[512,512]{1,0:T(8,128)S(1)} %fusion.10) | copy-start | bytes 3145732
Sparse Core Ops, SparseCore 0:
  464.9 96.8 reduce-scatter.3
  564.1 71.7 all-gather.1
  638.7 56.5 all-reduce.3
  697.8 61.9 all-reduce.5
where the time goes:
time: 928 us; the launch traced here: 923 us
  local copies, waits for them, and re-layouts  402 us (43%)
  waiting for transfers between devices  323 us (35%)
  other arithmetic  129 us (14%)
  matrix products  18.6 us (2%)
  between operations  17.2 us (2%)
  starting transfers between devices  16.9 us (2%)
  blocking collectives  16.2 us (2%)
    gather x3, local copies, waits for them, and re-layouts, body(): taken = gmap[operation[:, None], columns[None, :]]  258 us
    gather x2, local copies, waits for them, and re-layouts, body(): picked = jnp.take(own_rows, taken, axis=1)  121 us
    psum x2, waiting for transfers between devices, broadcast(): return lax.psum(block, axis)  103 us
    unnamed x5, waiting for transfers between devices  93.2 us
    another operation x15, other arithmetic, body(): factor = jnp.linalg.cholesky(diagonal)  79.4 us
    all_gather x1, waiting for transfers between devices, body(): gathered = lax.all_gather(eps_rows, 'kb', axis=0, tiled=True)  72.2 us
    all_to_all x1, waiting for transfers between devices, body(): lax.all_to_all(outgoing, 'kb', split_axis=1, concat_axis=1, tiled=True)  55.2 us
    another operation x4, other arithmetic, body(): lax.linalg.triangular_solve(factor, left_rows, left_side=False, lower=Tru...  41.4 us
  transfers between devices with their start and end apart: 5, of which 5 were waited for; matrix products, arithmetic and copies ran while one was open for 0% of the time, Pallas kernels for 0%

commit v1 on v0

v1 whole, which is shorter than its diff:
```python
import functools
import jax
import jax.numpy as jnp
from jax import lax
from jax.experimental import pallas as pl
from jax.experimental.pallas import tpu as pltpu
from jax.sharding import PartitionSpec as P

MESH = pl.DeviceIdType.MESH
HI = lax.Precision.HIGHEST
NT = (((1,), (1,)), ((), ()))
TN = (((0,), (0,)), ((), ()))
LOW = 256
BLOCK = 128


def product(a, b, dims=(((1,), (0,)), ((), ()))):
    return lax.dot_general(a, b, dims, precision=HI, preferred_element_type=jnp.float32)


def inverse_factor(d, hook):
    n = d.shape[0]
    lane = lax.broadcasted_iota(jnp.int32, (8, n), 1)
    sub = lax.broadcasted_iota(jnp.int32, (8, n), 0)
    tail = d.reshape(n // 8, 8, n)
    out = []
    for g in range(n // 8):
        base = 8 * g
        hook(g)
        cols = [jnp.broadcast_to(tail[:, :, base + k:base + k + 1], tail.shape) for k in range(8)]
        inside = (lane >= base) & (lane < base + 8)
        head = jnp.where(inside, jnp.where(lane - base == sub, 1.0, 0.0), tail[0])
        rest = jnp.where(inside[None], 0.0, tail[1:]) if g + 1 < n // 8 else None
        entry = {(i, k): jnp.broadcast_to(cols[k][0, i:i + 1, :], (8, n)) for i in range(8) for k in range(i + 1)}
        row = [jnp.broadcast_to(head[i:i + 1, :], (8, n)) for i in range(8)]
        below = [c[1:] for c in cols]
        done = jnp.zeros((8, n), jnp.float32)
        for j in range(8):
            scale = lax.rsqrt(entry[j, j])
            pivot_row = row[j] * scale
            done = jnp.where(sub == j, pivot_row, done)
            mult = {i: entry[i, j] * scale for i in range(j + 1, 8)}
            for i in range(j + 1, 8):
                row[i] = row[i] - mult[i] * pivot_row
                for k in range(j + 1, i + 1):
                    entry[i, k] = entry[i, k] - mult[i] * mult[k]
            if rest is not None:
                step = below[j] * scale[None]
                rest = rest - step * pivot_row[None]
                for k in range(j + 1, 8):
                    below[k] = below[k] - step * mult[k][None]
        out.append(jnp.where(lane <= sub + base, done, 0.0))
        tail = rest
    return jnp.concatenate(out, axis=0)


def whole_kernel(chips, grid, wedge_ref, op_ref, x_ref, ec_ref, ev_ref, coulomb_ref, gmap_ref, out_ref,
                 lo_ref, hi_ref, s_ref, y_ref, p_ref, c1_recv, c2_send, c2_recv, e00_ref, total_ref,
                 pair_ref, send_ref, recv_ref, far_send_ref, far_recv_ref, f_ref, own_ref, left_ref, top_ref,
                 r_ref, inv_ref, low_ref, w_ref,
                 c1_s, c1_r, c2_s, c2_r, c3_s, c3_r, c4_s, c4_r, c5_s, c5_r,
                 pair_s, pair_r, near_s, near_r, far_s, far_r, swap_s, swap_r,
                 top_s, top_r, side_s, side_r, ag_s, ag_r, fw_s, fw_r):
    kb, gr, gc = lax.axis_index("kb"), lax.axis_index("gr"), lax.axis_index("gc")
    z, c = kb // 2, kb % 2
    other = 1 - c
    owners, slots = wedge_ref.shape
    bands, total_g = x_ref.shape
    band, width = out_ref.shape
    rows, wide = 2 * band, width // 2
    is_top, is_left = gr == 0, gc == 0

    def chip(delta, core=None):
        return (2 * ((z + delta + chips) % chips) + (c if core is None else core), gr, gc)

    def remote(src, dst, send, recv, who):
        return pltpu.make_async_remote_copy(
            src_ref=src, dst_ref=dst, send_sem=send, recv_sem=recv, device_id=who, device_id_type=MESH
        )

    partner = (2 * z + other, gr, gc)
    peers = {
        i: (kb, (gr + i // grid) % grid, (gc + i % grid) % grid) for i in range(1, grid * grid)
    }
    barrier = pltpu.get_barrier_semaphore()
    everyone = (
        [chip(d, core) for d in (1, -1, 2, -2) for core in (0, 1)]
        + [chip(d) for d in (4, -4, 8)] + [partner] + list(peers.values())
    )
    for who in everyone:
        pl.semaphore_signal(barrier, inc=1, device_id=who, device_id_type=MESH)

    eye = lax.broadcasted_iota(jnp.int32, (bands, bands), 0) == lax.broadcasted_iota(jnp.int32, (bands, bands), 1)
    gap = ec_ref[...] - ev_ref[...]
    weight = jnp.sqrt(4.0 / (float(owners * slots) * gap))
    weight = jnp.sum(jnp.where(eye, jnp.broadcast_to(weight, (bands, bands)), 0.0), axis=1, keepdims=True)
    y = (x_ref[...].astype(jnp.float32) * weight).astype(jnp.bfloat16)
    parts = total_g // LOW
    for h in range(parts):
        y_ref[h * bands:(h + 1) * bands, :] = y[:, h * LOW:(h + 1) * LOW]
    matched = jnp.where(wedge_ref[...] == kb, 1.0, 0.0)
    present = jnp.sum(matched, axis=1, keepdims=True)
    operation = jnp.sum(matched * op_ref[...].astype(jnp.float32), axis=1, keepdims=True).astype(jnp.int32)
    kinds = lax.broadcasted_iota(jnp.int32, (owners, gmap_ref.shape[0]), 1)
    chosen = jnp.where(kinds == operation, present, 0.0).astype(jnp.bfloat16)
    count = lax.broadcasted_iota(jnp.int32, (LOW, 128), 0).astype(jnp.float32).astype(jnp.bfloat16)
    one, none = jnp.ones((LOW, 128), jnp.bfloat16), jnp.zeros((LOW, 128), jnp.bfloat16)

    def gather(side, at):
        maps = gmap_ref[:, pl.ds(at, width)]
        low_bits = (maps & (LOW - 1)).astype(jnp.float32).astype(jnp.bfloat16)
        high_bits = (maps >> (LOW.bit_length() - 1)).astype(jnp.float32).astype(jnp.bfloat16)
        lo_ref[...] = jnp.dot(chosen, low_bits, preferred_element_type=jnp.float32)
        hi_ref[...] = jnp.dot(chosen, high_bits, preferred_element_type=jnp.float32) + (present - 1.0)

        def pick(o, carry):
            low = jnp.broadcast_to(lo_ref[pl.ds(o, 1), :], (LOW, width)).astype(jnp.bfloat16)
            high = hi_ref[pl.ds(o, 1), :]
            onehot = jnp.concatenate(
                [jnp.where(count == low[:, t:t + 128], one, none) for t in range(0, width, 128)], axis=1
            )
            spread = jnp.dot(y_ref[...], onehot, preferred_element_type=jnp.float32)
            picked = jnp.zeros((bands, width), jnp.float32)
            for h in range(parts):
                picked = jnp.where(high == float(h), spread[h * bands:(h + 1) * bands, :], picked)
            s_ref[pl.ds(pl.multiple_of(o * bands, bands), bands), side * width:(side + 1) * width] = picked.astype(jnp.bfloat16)
            return carry

        lax.fori_loop(0, owners, pick, 0, unroll=4)

    root = jnp.sqrt(coulomb_ref[...])

    def root_down(first, count, reach):
        ids = first + lax.broadcasted_iota(jnp.int32, (count, reach), 0)
        lanes = lax.broadcasted_iota(jnp.int32, (count, reach), 1)
        return jnp.sum(jnp.where(ids == lanes, jnp.broadcast_to(root[:, :reach], (count, reach)), 0.0), axis=1, keepdims=True)

    def dielectric(value, first_row, first_col):
        count, across = value.shape
        reach = total_g
        row = first_row + lax.broadcasted_iota(jnp.int32, (count, across), 0)
        col = first_col + lax.broadcasted_iota(jnp.int32, (count, across), 1)
        root_across = jnp.sqrt(coulomb_ref[:, pl.ds(pl.multiple_of(first_col, 128), across)])
        return jnp.where(row == col, 1.0, 0.0) + root_down(first_row, count, reach) * value * root_across

    gather(0, 0)
    p_ref[...] = lax.dot_general(
        s_ref[:, pl.ds(pl.multiple_of(gr * BLOCK, BLOCK), BLOCK)], s_ref[:, :width], TN, preferred_element_type=jnp.float32
    )
    pl.semaphore_wait(barrier, len(everyone))

    def p_part(delta, core):
        k = (z + delta + chips) % grid
        return p_ref.at[pl.ds(pl.multiple_of(gc * rows + 8 * k, 8), 8), pl.ds(pl.multiple_of(core * wide, wide), wide)]

    near_parts = [(1, 0, c), (1, 1, c), (-1, 0, 2 + c), (-1, 1, 2 + c), (2, 0, 4 + c), (-2, 1, 4 + c), (0, other, 6)]
    stage1 = [
        remote(p_part(d, core), c1_recv.at[slot], c1_s.at[i], c1_r.at[slot], chip(d, core))
        for i, (d, core, slot) in enumerate(near_parts)
    ]
    for copy in stage1:
        copy.start()

    gather(1, pl.multiple_of(gr * width, width))

    value = p_part(0, c)[...]
    for slot in range(7):
        remote(p_part(0, other), c1_recv.at[slot], c1_s.at[0], c1_r.at[slot], partner).wait_recv()
        value = value + c1_recv[slot]
    c2_send[...] = value
    stage2 = [
        remote(c2_send, c2_recv.at[i], c2_s.at[i], c2_r.at[i], chip(d)) for i, d in enumerate((8, 4, -4))
    ]
    for copy in stage2:
        copy.start()

    gather(2, pl.multiple_of(gc * width, width))

    mine = pl.ds(pl.multiple_of(c * wide, wide), wide)
    theirs = pl.ds(pl.multiple_of(other * wide, wide), wide)
    total_ref[...] = lax.dot_general(
        s_ref[:, width:2 * width], s_ref[:, 2 * width:], TN, preferred_element_type=jnp.float32
    )

    def chunk(off):
        return pl.ds(pl.multiple_of(((z + off + chips) % chips) * rows, rows), rows)

    near = [
        (9, 1, 2), (7, -1, 6), (5, 1, 1), (3, -1, 5), (6, 2, 9), (-6, -2, 11),
        (13, 1, 3), (11, -1, 7), (1, 1, 0), (15, -1, 4), (2, 2, 8), (-2, -2, 10),
    ]
    order = [off % chips for off, _, _ in near] + [8, 4, 12, 0]
    pairs = {
        off: remote(total_ref.at[chunk(off), theirs], pair_ref.at[i], pair_s.at[i], pair_r.at[i], partner)
        for i, off in enumerate(order)
    }
    for off in order:
        pairs[off].start()

    value = c2_send[...]
    for i in (1, 2, 0):
        stage2[i].wait_recv()
        value = value + c2_recv[i]
    first = gr * BLOCK + gc * rows
    first_e = pl.multiple_of(first + 8 * (z % grid), 8)
    part = e00_ref.at[pl.ds(first_e, 8), mine]
    part[...] = dielectric(value, first_e, c * wide)
    two = jnp.where(c == 0, 2, -2)
    spread_to = [(1, 0, c), (1, 1, c), (-1, 0, 2 + c), (-1, 1, 2 + c), (two, 0, 4 + c), (two, 1, 4 + c), (0, other, 6)]
    stage3 = [
        remote(part, part, c3_s.at[i], c3_r.at[slot], chip(d, core)) for i, (d, core, slot) in enumerate(spread_to)
    ]
    for copy in stage3:
        copy.start()

    def own_part(off):
        off = off % chips
        pairs[off].wait_recv()
        return total_ref[chunk(off), mine] + pair_ref[order.index(off)]

    near_copies = {}
    for off, delta, slot in near:
        send_ref[slot] = own_part(off)
        copy = remote(send_ref.at[slot], recv_ref.at[slot], near_s.at[slot], near_r.at[slot], chip(delta))
        copy.start()
        near_copies[slot] = copy

    for slot in range(7):
        remote(part, part, c3_s.at[0], c3_r.at[slot], partner).wait_recv()

    def e00_part(r, s, half):
        return e00_ref.at[pl.ds(pl.multiple_of(r * BLOCK + s * rows, rows), rows), half]

    def needed(r, core):
        return jnp.logical_or(core == 1, r < 2)

    def stage4(i):
        return remote(e00_part(gr, gc, mine), e00_part(gr, gc, mine), c4_s.at[i], c4_r.at[i], peers[i])

    def sender(i):
        return (gr + grid - i // grid) % grid, (gc + grid - i % grid) % grid

    @pl.when(needed(gr, c))
    def _():
        for i in peers:
            stage4(i).start()

    def stage5(i, half):
        r, s = sender(i)
        return remote(e00_part(r, s, half), e00_part(r, s, half), c5_s.at[i], c5_r.at[i], partner)

    for i in peers:
        @pl.when(needed(sender(i)[0], c))
        def _():
            stage4(i).wait_recv()
            stage5(i, mine).start()
    def gathered(j, extra):
        value = own_part(4 * j)
        for slot in (j, 4 + j) + extra:
            near_copies[slot].wait_recv()
            value = value + recv_ref[slot]
        return value

    far_list = [(2, (), 8), (1, (9,), 4), (3, (11,), -4)]

    def far_copy(i):
        return remote(far_send_ref.at[i], far_recv_ref.at[i], far_s.at[i], far_r.at[i], chip(far_list[i][2]))

    def end_e00_copies():
        for copy in stage3:
            copy.wait_send()

        @pl.when(needed(gr, c))
        def _():
            for i in peers:
                stage4(i).wait_send()
        for i in peers:
            @pl.when(needed(sender(i)[0], c))
            def _():
                stage5(i, mine).wait_send()

    def send_far():
        for i, (j, extra, delta) in enumerate(far_list):
            far_send_ref[i] = gathered(j, extra)
            far_copy(i).start()

    my_top = top_ref.at[chunk(0), mine]

    def to_top(i):
        return remote(f_ref, my_top, top_s.at[i - 1], top_r, (kb, (gr + i) % grid, gc))

    swap = remote(f_ref.at[pl.ds(pl.multiple_of(other * band, band), band)], own_ref.at[:, mine], swap_s, swap_r, partner)

    def send_top():
        value = gathered(0, (8, 10))
        for i in (1, 2, 0):
            far_copy(i).wait_recv()
            value = value + far_recv_ref[i]
        value = dielectric(value, gr * width + z * rows, gc * width + c * wide)
        f_ref[...] = value

        @pl.when(is_top)
        def _():
            for i in range(1, grid):
                to_top(i).start()
            my_top[...] = value

        swap.start()
        own_ref[:, mine] = f_ref[pl.ds(pl.multiple_of(c * band, band), band)]

    def piece(off):
        return top_ref.at[chunk(off), mine]

    def forward(off):
        return remote(piece(off), piece(off), fw_s.at[off], fw_r.at[off], partner)

    gossip = {
        0: ((8, 0), (4, 1), (-4, 2), (1, 3), (-1, 4), (2, 5), (-2, 6)),
        4: ((1, 7), (-1, 8), (-2, 9)),
        12: ((1, 10), (-1, 11), (2, 12)),
        8: ((1, 13), (-1, 14)),
    }

    def gossip_copy(off, delta, i):
        return remote(piece(off), piece(off), ag_s.at[i], ag_r.at[(off - delta) % chips], chip(delta))

    def arrive(off):
        remote(piece(off), piece(off), ag_s.at[0], ag_r.at[off], partner).wait_recv()

    def to_side(i):
        return remote(own_ref, left_ref, side_s.at[i - 1], side_r, (kb, gr, (gc + i) % grid))

    def send_first():
        @pl.when(jnp.logical_not(is_top))
        def _():
            to_top(1).wait_recv()

        for delta, i in gossip[0]:
            gossip_copy(0, delta, i).start()
        forward(0).start()
        swap.wait_recv()

        @pl.when(is_left)
        def _():
            for i in range(1, grid):
                to_side(i).start()

    def send_second():
        for off in (4, 12, 8):
            arrive(off)
            for delta, i in gossip[off]:
                gossip_copy(off, delta, i).start()
            forward(off).start()

    send_far()
    for i in peers:
        @pl.when(needed(sender(i)[0], other))
        def _():
            stage5(i, theirs).wait_recv()

    plan = {(0, 15): end_e00_copies, (1, 6): send_top, (2, 2): send_first, (3, 8): send_second}
    cuts = [slice(b * BLOCK, (b + 1) * BLOCK) for b in range(width // BLOCK)]
    for b, cut in enumerate(cuts):
        def hook(g):
            if (b, g) in plan:
                plan[b, g]()

        inverse = inverse_factor(e00_ref[cut, cut], hook)
        inv_ref[cut, :] = inverse
        after = (b + 1) * BLOCK
        if after < width:
            across = product(inverse, e00_ref[cut, after:])
            r_ref[cut, after:] = across
            for cut2 in cuts[b + 1:]:
                at = cut2.start
                e00_ref[cut2, at:] = e00_ref[cut2, at:] - product(
                    across[:, at - after:at - after + BLOCK], across[:, at - after:], TN
                )

    @pl.when(jnp.logical_not(is_left))
    def _():
        to_side(1).wait_recv()

    @pl.when(is_left)
    def _():
        left_ref[...] = own_ref[...]

    for b, cut in enumerate(cuts):
        value = left_ref[:, cut]
        if b:
            value = value - product(low_ref[:, :b * BLOCK], r_ref[:b * BLOCK, cut])
        low_ref[:, cut] = product(value, inv_ref[cut, :], NT)
    for b in reversed(range(len(cuts))):
        cut = cuts[b]
        value = low_ref[:, cut]
        if b + 1 < len(cuts):
            value = value - product(w_ref[:, (b + 1) * BLOCK:], r_ref[cut, (b + 1) * BLOCK:], NT)
        w_ref[:, cut] = product(value, inv_ref[cut, :])

    for off in (1, 15, 2, 14, 5, 3, 13, 11, 6, 10, 7, 9):
        arrive(off)
        forward(off).start()
    for off in range(chips):
        forward(off).wait_recv()

    row = kb * band + lax.broadcasted_iota(jnp.int32, (band, width), 0)
    col = lax.broadcasted_iota(jnp.int32, (band, width), 1)
    factor_side = jnp.where(is_top & (col > row), 0.0, low_ref[...])
    trail = own_ref[...] - product(w_ref[...], top_ref[...])
    out_ref[...] = jnp.where(is_left, factor_side, jnp.where(is_top, own_ref[...], trail))

    for copy in stage1 + stage2 + list(pairs.values()) + list(near_copies.values()) + [swap]:
        copy.wait_send()
    for i in range(3):
        far_copy(i).wait_send()
    for off, sends in gossip.items():
        for delta, i in sends:
            gossip_copy(off, delta, i).wait_send()
    for off in range(chips):
        forward(off).wait_send()

    @pl.when(is_top)
    def _():
        for i in range(1, grid):
            to_top(i).wait_send()

    @pl.when(is_left)
    def _():
        for i in range(1, grid):
            to_side(i).wait_send()


def body(wedge_pairs, e_cond, e_val, coulomb, owned_wedge, owned_op, gmap):
    members = lax.axis_size("kb")
    grid = lax.axis_size("gr")
    chips = members // 2
    total_g = gmap.shape[1]
    width = total_g // grid
    band = width // members
    owners = owned_wedge.shape[0]
    x = wedge_pairs.reshape(-1, total_g)
    bands = x.shape[0]
    vmem = pl.BlockSpec(memory_space=pltpu.VMEM)
    dma = pltpu.SemaphoreType.DMA
    piece = (2 * band, width // 2)
    f32 = jnp.float32
    return pl.pallas_call(
        functools.partial(whole_kernel, chips, grid),
        out_shape=jax.ShapeDtypeStruct((band, width), f32),
        in_specs=[vmem] * 7,
        out_specs=vmem,
        scratch_shapes=[
            pltpu.VMEM((owners, width), f32),
            pltpu.VMEM((owners, width), f32),
            pltpu.VMEM((owners * bands, 3 * width), jnp.bfloat16),
            pltpu.VMEM((bands * (total_g // LOW), LOW), jnp.bfloat16),
            pltpu.VMEM((BLOCK, width), f32),
            pltpu.VMEM((7, 8, width // 2), f32),
            pltpu.VMEM((8, width // 2), f32),
            pltpu.VMEM((3, 8, width // 2), f32),
            pltpu.VMEM((width, width), f32),
            pltpu.VMEM((width, width), f32),
            pltpu.VMEM((chips,) + piece, f32),
            pltpu.VMEM((12,) + piece, f32),
            pltpu.VMEM((12,) + piece, f32),
            pltpu.VMEM((3,) + piece, f32),
            pltpu.VMEM((3,) + piece, f32),
            pltpu.VMEM(piece, f32),
            pltpu.VMEM((band, width), f32),
            pltpu.VMEM((band, width), f32),
            pltpu.VMEM((width, width), f32),
            pltpu.VMEM((width, width), f32),
            pltpu.VMEM((width, BLOCK), f32),
            pltpu.VMEM((band, width), f32),
            pltpu.VMEM((band, width), f32),
            dma((7,)), dma((7,)),
            dma((3,)), dma((3,)),
            dma((7,)), dma((7,)),
            dma((grid * grid,)), dma((grid * grid,)),
            dma((grid * grid,)), dma((grid * grid,)),
            dma((chips,)), dma((chips,)),
            dma((12,)), dma((12,)),
            dma((3,)), dma((3,)),
            dma, dma,
            dma((grid - 1,)), dma,
            dma((grid - 1,)), dma,
            dma((15,)), dma((chips,)),
            dma((chips,)), dma((chips,)),
        ],
        compiler_params=pltpu.CompilerParams(
            collective_id=0, has_side_effects=True, vmem_limit_bytes=40 << 20
        ),
        name="whole",
    )(owned_wedge, owned_op, x, e_cond, e_val, coulomb.reshape(1, -1), gmap)


def solution(mesh):
    placed = (P("kb", None, None, None), P("kb", None), P("kb", None), P(), P(), P(), P())
    return jax.shard_map(
        body, mesh=mesh, in_specs=placed, out_specs=P(("gr", "kb"), "gc"), check_vma=False
    )
```

time: 928 us -> 77.7 us (0.08)
  local copies, waits for them, and re-layouts: 402 us -> 3.94 us
  waiting for transfers between devices: 323 us -> 0 us
  other arithmetic: 129 us -> 0 us
  Pallas kernels: 0 us -> 72.6 us
  matrix products: 18.6 us -> 0 us
  starting transfers between devices: 16.9 us -> 0 us
  between operations: 17.2 us -> 0.68 us
  blocking collectives: 16.2 us -> 0 us
    gather x10 -> x0, local copies, waits for them, and re-layouts: 384 us -> none  [the longest x3 258 us: body(): taken = gmap[operation[:, None], columns[None, :]]]
    another operation x19 -> x0, other arithmetic: 121 us -> none  [the longest x15 79.4 us: body(): factor = jnp.linalg.cholesky(diagonal)]
    psum x2 -> x0, waiting for transfers between devices: 103 us -> none  [broadcast(): return lax.psum(block, axis)]
    unnamed x5 -> x0, waiting for transfers between devices: 93.2 us -> none
    pallas_call x0 -> x1, Pallas kernels: none -> 72.6 us  [body(): pl.pallas_call(functools.partial(whole_kernel, chips, grid), out_shape=ja...]
    all_gather x1 -> x0, waiting for transfers between devices: 72.2 us -> none  [body(): gathered = lax.all_gather(eps_rows, 'kb', axis=0, tiled=True)]
    all_to_all x1 -> x0, waiting for transfers between devices: 55.2 us -> none  [body(): lax.all_to_all(outgoing, 'kb', split_axis=1, concat_axis=1, tiled=True)]
    all_to_all x1 -> x0, starting transfers between devices: 16.8 us -> none  [body(): lax.all_to_all(outgoing, 'kb', split_axis=1, concat_axis=1, tiled=True)]
  transfers between devices with their start and end apart: 5 -> 0, of which waited for: 5 -> 0; matrix products, arithmetic and copies ran while one was open for 0% -> 0% of each run, Pallas kernels for 0% -> 0%
where the time goes in v1:
time: 77.7 us; the launch traced here: 77.2 us
  Pallas kernels  72.6 us (93%)
  local copies, waits for them, and re-layouts  3.94 us (5%)
    pallas_call x1, Pallas kernels, body(): pl.pallas_call(functools.partial(whole_kernel, chips, grid), out_shape=ja...  72.6 us
    unnamed x13, local copies, waits for them, and re-layouts  3.94 us

profile of v1, /device:TPU:1, one launch (start us, length us, event | category | flops | bytes accessed | tf_op | source)
XLA Modules:
  0.0 77.2 jit_solution(4620698851011756858)
XLA Ops:
  0.7 0.0 copy-start.4
  0.7 0.8 %copy.8.wedge_ref = s32[32,17]{1,0:T(8,128)S(1)} copy(s32[32,17]{0,1:T(8,128)} %param.11) | data formatting | bytes 4352 | tf_op args[4]
  1.5 0.0 copy-done.4
  1.5 0.0 copy-start.2
  1.5 0.0 copy-start.3
  1.5 0.1 copy.9.op_ref
  1.5 0.6 copy-done.2
  2.2 0.0 copy-done.3
  2.2 0.0 copy-start
  2.2 1.0 %copy-done = s32[48,2048]{1,0:T(8,128)S(1)} copy-done((s32[48,2048]{1,0:T(8,128)S(1)}, s32[48,2048]{1,0:T(8,128)}, u32[]{:S(2)}) %copy-start) | copy-done | bytes 393240
  3.2 0.0 copy-start.1
  3.2 0.8 %copy-done.1 = bf16[1,1,16,2048]{3,2,1,0:T(8,128)(2,1)S(1)} copy-done((bf16[1,1,16,2048]{3,2,1,0:T(8,128)(2,1)S(1)}, bf16[1,1,16,2048]{3,2,1,0:T(8,128)(2,1)}, u32[]{:S(2)}) %copy-start.1) | copy-done | bytes 65560
  4.0 72.6 %whole.1 = f32[16,512]{1,0:T(8,128)S(1)} custom-call(s32[32,17]{1,0:T(8,128)S(1)} %copy.8.wedge_ref, s32[32,17]{1,0:T(8,128)S(1)} %copy.9.op_ref, bf16[16,2048]{1,0:T(8,128)(2,1)S(1)} %bitcast.2, f32[1,1]{1,0:T(1,128)S(6)} %copy.11.ec_ref, f32[1,16]{1,0:T(1,128)S(1)} %copy-done.3, f32[1,2048]{1,0:T(1,128)S(1)} %bitcast.3, s32[48,2048]{1,0:T(8,128)S(1)} %copy-done), custom_call_target="tpu_custom_call" | custom-call | tf_op jit(solution)/shard_map/whole/pallas_call | solution.py:447
  76.6 0.6 copy.12
Async XLA Ops:
  0.7 0.8 %copy-start.4 = (s32[32,17]{0,1:T(8,128)S(1)}, s32[32,17]{0,1:T(8,128)}, u32[]{:S(2)}) copy-start(s32[32,17]{0,1:T(8,128)} %param.12) | copy-start | bytes 6532
  1.5 0.7 copy-start.2
  1.5 0.7 copy-start.3
  2.2 1.0 %copy-start = (s32[48,2048]{1,0:T(8,128)S(1)}, s32[48,2048]{1,0:T(8,128)}, u32[]{:S(2)}) copy-start(s32[48,2048]{1,0:T(8,128)} %gmap_ref.1) | copy-start | bytes 1179652
  3.2 0.8 %copy-start.1 = (bf16[1,1,16,2048]{3,2,1,0:T(8,128)(2,1)S(1)}, bf16[1,1,16,2048]{3,2,1,0:T(8,128)(2,1)}, u32[]{:S(2)}) copy-start(bf16[1,1,16,2048]{3,2,1,0:T(8,128)(2,1)} %param.7) | copy-start | bytes 196612

commit v2 on v1

--- a/solution.py
+++ b/solution.py
@@ -54,21 +54,31 @@
     return jnp.concatenate(out, axis=0)
 
 
-def whole_kernel(chips, grid, wedge_ref, op_ref, x_ref, ec_ref, ev_ref, coulomb_ref, gmap_ref, out_ref,
+def whole_kernel(chips, grid, wedge_hbm, op_hbm, x_hbm, ec_ref, ev_ref, coulomb_hbm, gmap_hbm, out_ref,
+                 wedge_ref, op_ref, x_ref, coulomb_ref, gmap_ref, scale_ref, g_ref,
                  lo_ref, hi_ref, s_ref, y_ref, p_ref, c1_recv, c2_send, c2_recv, e00_ref, total_ref,
                  pair_ref, send_ref, recv_ref, far_send_ref, far_recv_ref, f_ref, own_ref, left_ref, top_ref,
-                 r_ref, inv_ref, low_ref, w_ref,
+                 low_ref, w_ref,
                  c1_s, c1_r, c2_s, c2_r, c3_s, c3_r, c4_s, c4_r, c5_s, c5_r,
                  pair_s, pair_r, near_s, near_r, far_s, far_r, swap_s, swap_r,
-                 top_s, top_r, side_s, side_r, ag_s, ag_r, fw_s, fw_r):
+                 top_s, top_r, side_s, side_r, ag_s, ag_r, fw_s, fw_r, in_s):
     kb, gr, gc = lax.axis_index("kb"), lax.axis_index("gr"), lax.axis_index("gc")
     z, c = kb // 2, kb % 2
     other = 1 - c
-    owners, slots = wedge_ref.shape
+    slots, owners = wedge_ref.shape
     bands, total_g = x_ref.shape
     band, width = out_ref.shape
     rows, wide = 2 * band, width // 2
     is_top, is_left = gr == 0, gc == 0
+
+    fetched = [
+        pltpu.make_async_copy(src, dst, in_s.at[i])
+        for i, (src, dst) in enumerate([
+            (gmap_hbm, gmap_ref), (x_hbm, x_ref), (wedge_hbm, wedge_ref), (op_hbm, op_ref), (coulomb_hbm, coulomb_ref)
+        ])
+    ]
+    for copy in fetched:
+        copy.start()
 
     def chip(delta, core=None):
         return (2 * ((z + delta + chips) % chips) + (c if core is None else core), gr, gc)
@@ -90,6 +100,9 @@
     for who in everyone:
         pl.semaphore_signal(barrier, inc=1, device_id=who, device_id_type=MESH)
 
+    for copy in fetched:
+        copy.wait()
+
     eye = lax.broadcasted_iota(jnp.int32, (bands, bands), 0) == lax.broadcasted_iota(jnp.int32, (bands, bands), 1)
     gap = ec_ref[...] - ev_ref[...]
     weight = jnp.sqrt(4.0 / (float(owners * slots) * gap))
@@ -99,9 +112,9 @@
     for h in range(parts):
         y_ref[h * bands:(h + 1) * bands, :] = y[:, h * LOW:(h + 1) * LOW]
     matched = jnp.where(wedge_ref[...] == kb, 1.0, 0.0)
-    present = jnp.sum(matched, axis=1, keepdims=True)
-    operation = jnp.sum(matched * op_ref[...].astype(jnp.float32), axis=1, keepdims=True).astype(jnp.int32)
-    kinds = lax.broadcasted_iota(jnp.int32, (owners, gmap_ref.shape[0]), 1)
+    present = jnp.sum(matched, axis=0, keepdims=True)
+    operation = jnp.sum(matched * op_ref[...].astype(jnp.float32), axis=0, keepdims=True)
+    kinds = lax.broadcasted_iota(jnp.int32, (gmap_ref.shape[0], owners), 0).astype(jnp.float32)
     chosen = jnp.where(kinds == operation, present, 0.0).astype(jnp.bfloat16)
     count = lax.broadcasted_iota(jnp.int32, (LOW, 128), 0).astype(jnp.float32).astype(jnp.bfloat16)
     one, none = jnp.ones((LOW, 128), jnp.bfloat16), jnp.zeros((LOW, 128), jnp.bfloat16)
@@ -109,9 +122,9 @@
     def gather(side, at):
         maps = gmap_ref[:, pl.ds(at, width)]
         low_bits = (maps & (LOW - 1)).astype(jnp.float32).astype(jnp.bfloat16)
-        high_bits = (maps >> (LOW.bit_length() - 1)).astype(jnp.float32).astype(jnp.bfloat16)
-        lo_ref[...] = jnp.dot(chosen, low_bits, preferred_element_type=jnp.float32)
-        hi_ref[...] = jnp.dot(chosen, high_bits, preferred_element_type=jnp.float32) + (present - 1.0)
+        high_bits = ((maps >> (LOW.bit_length() - 1)) + 1).astype(jnp.float32).astype(jnp.bfloat16)
+        lo_ref[...] = lax.dot_general(chosen, low_bits, TN, preferred_element_type=jnp.float32)
+        hi_ref[...] = lax.dot_general(chosen, high_bits, TN, preferred_element_type=jnp.float32)
 
         def pick(o, carry):
             low = jnp.broadcast_to(lo_ref[pl.ds(o, 1), :], (LOW, width)).astype(jnp.bfloat16)
@@ -122,7 +135,7 @@
             spread = jnp.dot(y_ref[...], onehot, preferred_element_type=jnp.float32)
             picked = jnp.zeros((bands, width), jnp.float32)
             for h in range(parts):
-                picked = jnp.where(high == float(h), spread[h * bands:(h + 1) * bands, :], picked)
+                picked = jnp.where(high == float(h + 1), spread[h * bands:(h + 1) * bands, :], picked)
             s_ref[pl.ds(pl.multiple_of(o * bands, bands), bands), side * width:(side + 1) * width] = picked.astype(jnp.bfloat16)
             return carry
 
@@ -135,13 +148,15 @@
         lanes = lax.broadcasted_iota(jnp.int32, (count, reach), 1)
         return jnp.sum(jnp.where(ids == lanes, jnp.broadcast_to(root[:, :reach], (count, reach)), 0.0), axis=1, keepdims=True)
 
-    def dielectric(value, first_row, first_col):
-        count, across = value.shape
-        reach = total_g
-        row = first_row + lax.broadcasted_iota(jnp.int32, (count, across), 0)
-        col = first_col + lax.broadcasted_iota(jnp.int32, (count, across), 1)
-        root_across = jnp.sqrt(coulomb_ref[:, pl.ds(pl.multiple_of(first_col, 128), across)])
-        return jnp.where(row == col, 1.0, 0.0) + root_down(first_row, count, reach) * value * root_across
+    def scale_of(first_row, first_col, count, across):
+        return root_down(first_row, count, total_g) * jnp.sqrt(
+            coulomb_ref[:, pl.ds(pl.multiple_of(first_col, 128), across)]
+        )
+
+    def dielectric(value, scale, first_row, first_col):
+        row = first_row + lax.broadcasted_iota(jnp.int32, value.shape, 0)
+        col = first_col + lax.broadcasted_iota(jnp.int32, value.shape, 1)
+        return jnp.where(row == col, 1.0, 0.0) + scale * value
 
     gather(0, 0)
     p_ref[...] = lax.dot_general(
@@ -162,6 +177,10 @@
         copy.start()
 
     gather(1, pl.multiple_of(gr * width, width))
+    first_e = pl.multiple_of(gr * BLOCK + gc * rows + 8 * (z % grid), 8)
+    scale_e = scale_of(first_e, c * wide, 8, wide)
+    first_row, first_col = gr * width + z * rows, gc * width + c * wide
+    scale_ref[...] = scale_of(first_row, first_col, rows, wide)
 
     value = p_part(0, c)[...]
     for slot in range(7):
@@ -201,10 +220,8 @@
     for i in (1, 2, 0):
         stage2[i].wait_recv()
         value = value + c2_recv[i]
-    first = gr * BLOCK + gc * rows
-    first_e = pl.multiple_of(first + 8 * (z % grid), 8)
     part = e00_ref.at[pl.ds(first_e, 8), mine]
-    part[...] = dielectric(value, first_e, c * wide)
+    part[...] = dielectric(value, scale_e, first_e, c * wide)
     two = jnp.where(c == 0, 2, -2)
     spread_to = [(1, 0, c), (1, 1, c), (-1, 0, 2 + c), (-1, 1, 2 + c), (two, 0, 4 + c), (two, 1, 4 + c), (0, other, 6)]
     stage3 = [
@@ -249,11 +266,7 @@
         r, s = sender(i)
         return remote(e00_part(r, s, half), e00_part(r, s, half), c5_s.at[i], c5_r.at[i], partner)
 
-    for i in peers:
-        @pl.when(needed(sender(i)[0], c))
-        def _():
-            stage4(i).wait_recv()
-            stage5(i, mine).start()
+
     def gathered(j, extra):
         value = own_part(4 * j)
         for slot in (j, 4 + j) + extra:
@@ -296,7 +309,7 @@
         for i in (1, 2, 0):
             far_copy(i).wait_recv()
             value = value + far_recv_ref[i]
-        value = dielectric(value, gr * width + z * rows, gc * width + c * wide)
+        value = dielectric(value, scale_ref[...], first_row, first_col)
         f_ref[...] = value
 
         @pl.when(is_top)
@@ -354,11 +367,16 @@
 
     send_far()
     for i in peers:
+        @pl.when(needed(sender(i)[0], c))
+        def _():
+            stage4(i).wait_recv()
+            stage5(i, mine).start()
+    for i in peers:
         @pl.when(needed(sender(i)[0], other))
         def _():
             stage5(i, theirs).wait_recv()
 
-    plan = {(0, 15): end_e00_copies, (1, 6): send_top, (2, 2): send_first, (3, 8): send_second}
+    plan = {(0, 6): send_top, (0, 15): end_e00_copies, (1, 2): send_first, (3, 0): send_second}
     cuts = [slice(b * BLOCK, (b + 1) * BLOCK) for b in range(width // BLOCK)]
     for b, cut in enumerate(cuts):
         def hook(g):
@@ -366,16 +384,21 @@
                 plan[b, g]()
 
         inverse = inverse_factor(e00_ref[cut, cut], hook)
-        inv_ref[cut, :] = inverse
+        if b:
+            g_ref[cut, :b * BLOCK] = product(inverse, g_ref[cut, :b * BLOCK])
+        g_ref[cut, cut] = inverse
         after = (b + 1) * BLOCK
         if after < width:
             across = product(inverse, e00_ref[cut, after:])
-            r_ref[cut, after:] = across
             for cut2 in cuts[b + 1:]:
                 at = cut2.start
                 e00_ref[cut2, at:] = e00_ref[cut2, at:] - product(
                     across[:, at - after:at - after + BLOCK], across[:, at - after:], TN
                 )
+            change = product(across, g_ref[cut, :after], TN)
+            if b:
+                g_ref[after:, :cut.start] = g_ref[after:, :cut.start] - change[:, :cut.start]
+            g_ref[after:, cut] = -change[:, cut.start:]
 
     @pl.when(jnp.logical_not(is_left))
     def _():
@@ -385,17 +408,10 @@
     def _():
         left_ref[...] = own_ref[...]
 
-    for b, cut in enumerate(cuts):
-        value = left_ref[:, cut]
-        if b:
-            value = value - product(low_ref[:, :b * BLOCK], r_ref[:b * BLOCK, cut])
-        low_ref[:, cut] = product(value, inv_ref[cut, :], NT)
-    for b in reversed(range(len(cuts))):
-        cut = cuts[b]
-        value = low_ref[:, cut]
-        if b + 1 < len(cuts):
-            value = value - product(w_ref[:, (b + 1) * BLOCK:], r_ref[cut, (b + 1) * BLOCK:], NT)
-        w_ref[:, cut] = product(value, inv_ref[cut, :])
+    for cut in cuts:
+        low_ref[:, cut] = product(left_ref[:, :cut.stop], g_ref[cut, :cut.stop], NT)
+    for cut in cuts:
+        w_ref[:, cut] = product(low_ref[:, cut.start:], g_ref[cut.start:, cut])
 
     for off in (1, 15, 2, 14, 5, 3, 13, 11, 6, 10, 7, 9):
         arrive(off)
@@ -437,7 +453,8 @@
     total_g = gmap.shape[1]
     width = total_g // grid
     band = width // members
-    owners = owned_wedge.shape[0]
+    owners, slots = owned_wedge.shape
+    hbm = pl.BlockSpec(memory_space=pltpu.HBM)
     x = wedge_pairs.reshape(-1, total_g)
     bands = x.shape[0]
     vmem = pl.BlockSpec(memory_space=pltpu.VMEM)
@@ -447,9 +464,16 @@
     return pl.pallas_call(
         functools.partial(whole_kernel, chips, grid),
         out_shape=jax.ShapeDtypeStruct((band, width), f32),
-        in_specs=[vmem] * 7,
+        in_specs=[hbm] * 3 + [vmem] * 2 + [hbm] * 2,
         out_specs=vmem,
         scratch_shapes=[
+            pltpu.VMEM((slots, owners), jnp.int32),
+            pltpu.VMEM((slots, owners), jnp.int32),
+            pltpu.VMEM(x.shape, x.dtype),
+            pltpu.VMEM((1, total_g), f32),
+            pltpu.VMEM(gmap.shape, gmap.dtype),
+            pltpu.VMEM(piece, f32),
+            pltpu.VMEM((width, width), f32),
             pltpu.VMEM((owners, width), f32),
             pltpu.VMEM((owners, width), f32),
             pltpu.VMEM((owners * bands, 3 * width), jnp.bfloat16),
@@ -469,8 +493,6 @@
             pltpu.VMEM((band, width), f32),
             pltpu.VMEM((band, width), f32),
             pltpu.VMEM((width, width), f32),
-            pltpu.VMEM((width, width), f32),
-            pltpu.VMEM((width, BLOCK), f32),
             pltpu.VMEM((band, width), f32),
             pltpu.VMEM((band, width), f32),
             dma((7,)), dma((7,)),
@@ -486,12 +508,13 @@
             dma((grid - 1,)), dma,
             dma((15,)), dma((chips,)),
             dma((chips,)), dma((chips,)),
+            dma((5,)),
         ],
         compiler_params=pltpu.CompilerParams(
-            collective_id=0, has_side_effects=True, vmem_limit_bytes=40 << 20
+            collective_id=0, has_side_effects=True, vmem_limit_bytes=63 << 20
         ),
         name="whole",
-    )(owned_wedge, owned_op, x, e_cond, e_val, coulomb.reshape(1, -1), gmap)
+    )(owned_wedge.T, owned_op.T, x, e_cond, e_val, coulomb.reshape(1, -1), gmap)
 
 
 def solution(mesh):

time: 77.7 us -> 70.8 us (0.911)
  Pallas kernels: 72.6 us -> 68.6 us
  local copies, waits for them, and re-layouts: 3.94 us -> 1.38 us
    pallas_call x1, Pallas kernels: 72.6 us -> 68.6 us  [body(): pl.pallas_call(functools.partial(whole_kernel, chips, grid), out_shape=ja...]
    unnamed x13 -> x1, local copies, waits for them, and re-layouts: 3.94 us -> 1.38 us
where the time goes in v2:
time: 70.8 us; the launch traced here: 70.6 us
  Pallas kernels  68.6 us (97%)
  local copies, waits for them, and re-layouts  1.38 us (2%)
    pallas_call x1, Pallas kernels, body(): pl.pallas_call(functools.partial(whole_kernel, chips, grid), out_shape=ja...  68.6 us

profile of v2, /device:TPU:1, one launch (start us, length us, event | category | flops | bytes accessed | tf_op | source)
XLA Modules:
  0.0 70.6 jit_solution(13367386953399223478)
XLA Ops:
  0.7 68.6 %whole.1 = f32[16,512]{1,0:T(8,128)} custom-call(s32[17,32]{1,0:T(8,128)} %bitcast.5, s32[17,32]{1,0:T(8,128)} %bitcast.6, bf16[16,2048]{1,0:T(8,128)(2,1)} %bitcast.4, f32[1,1]{1,0:T(1,128)S(6)} %copy.9.ec_ref, f32[1,16]{1,0:T(1,128)} %ev_ref.1, f32[1,2048]{1,0:T(1,128)} %bitcast.7, s32[48,2048]{1,0:T(8,128)} %gmap_hbm.1), custom_call_target="tpu_custom_call" | custom-call | tf_op jit(solution)/shard_map/whole/pallas_call | solution.py:464
  69.2 1.4 %copy.10 = f32[16,512]{1,0:T(8,128)} copy(f32[16,512]{1,0:T(8,128)} %whole.1) | data formatting | bytes 65536

commit v3 on v2

--- a/solution.py
+++ b/solution.py
@@ -56,12 +56,12 @@
 
 def whole_kernel(chips, grid, wedge_hbm, op_hbm, x_hbm, ec_ref, ev_ref, coulomb_hbm, gmap_hbm, out_ref,
                  wedge_ref, op_ref, x_ref, coulomb_ref, gmap_ref, scale_ref, g_ref,
-                 lo_ref, hi_ref, s_ref, y_ref, p_ref, c1_recv, c2_send, c2_recv, e00_ref, total_ref,
+                 lo_ref, hi_ref, pt_ref, t1_recv, t2_send, t2_recv, t_scale_ref, s_ref, y_ref, p_ref, c1_recv, c2_send, c2_recv, e00_ref, total_ref,
                  pair_ref, send_ref, recv_ref, far_send_ref, far_recv_ref, f_ref, own_ref, left_ref, top_ref,
                  low_ref, w_ref,
                  c1_s, c1_r, c2_s, c2_r, c3_s, c3_r, c4_s, c4_r, c5_s, c5_r,
                  pair_s, pair_r, near_s, near_r, far_s, far_r, swap_s, swap_r,
-                 top_s, top_r, side_s, side_r, ag_s, ag_r, fw_s, fw_r, in_s):
+                 side_s, side_r, t1_s, t1_r, t2_s, t2_r, t3_s, t3_r, t4_s, t4_r, t5_s, t5_r, in_s):
     kb, gr, gc = lax.axis_index("kb"), lax.axis_index("gr"), lax.axis_index("gc")
     z, c = kb // 2, kb % 2
     other = 1 - c
@@ -176,11 +176,31 @@
     for copy in stage1:
         copy.start()
 
-    gather(1, pl.multiple_of(gr * width, width))
+    mine = pl.ds(pl.multiple_of(c * wide, wide), wide)
+    theirs = pl.ds(pl.multiple_of(other * wide, wide), wide)
+
+    gather(2, pl.multiple_of(gc * width, width))
+    pt_ref[...] = lax.dot_general(
+        s_ref[:, pl.ds(pl.multiple_of(gr * BLOCK, BLOCK), BLOCK)], s_ref[:, 2 * width:], TN, preferred_element_type=jnp.float32
+    )
+
+    def t_part(delta, core):
+        k = (z + delta + chips) % grid
+        return pt_ref.at[pl.ds(pl.multiple_of(rows * k, rows), rows), pl.ds(pl.multiple_of(core * wide, wide), wide)]
+
+    top1 = [
+        remote(t_part(d, core), t1_recv.at[slot], t1_s.at[i], t1_r.at[slot], chip(d, core))
+        for i, (d, core, slot) in enumerate(near_parts)
+    ]
+    for copy in top1:
+        copy.start()
+
     first_e = pl.multiple_of(gr * BLOCK + gc * rows + 8 * (z % grid), 8)
     scale_e = scale_of(first_e, c * wide, 8, wide)
     first_row, first_col = gr * width + z * rows, gc * width + c * wide
+    first_t = pl.multiple_of(gr * BLOCK + rows * (z % grid), rows)
     scale_ref[...] = scale_of(first_row, first_col, rows, wide)
+    t_scale_ref[...] = scale_of(first_t, first_col, rows, wide)
 
     value = p_part(0, c)[...]
     for slot in range(7):
@@ -193,10 +213,7 @@
     for copy in stage2:
         copy.start()
 
-    gather(2, pl.multiple_of(gc * width, width))
-
-    mine = pl.ds(pl.multiple_of(c * wide, wide), wide)
-    theirs = pl.ds(pl.multiple_of(other * wide, wide), wide)
+    gather(1, pl.multiple_of(gr * width, width))
     total_ref[...] = lax.dot_general(
         s_ref[:, width:2 * width], s_ref[:, 2 * width:], TN, preferred_element_type=jnp.float32
     )
@@ -230,6 +247,17 @@
     for copy in stage3:
         copy.start()
 
+    value = t_part(0, c)[...]
+    for slot in range(7):
+        remote(t_part(0, other), t1_recv.at[slot], t1_s.at[0], t1_r.at[slot], partner).wait_recv()
+        value = value + t1_recv[slot]
+    t2_send[...] = value
+    top2 = [
+        remote(t2_send, t2_recv.at[i], t2_s.at[i], t2_r.at[i], chip(d)) for i, d in enumerate((8, 4, -4))
+    ]
+    for copy in top2:
+        copy.start()
+
     def own_part(off):
         off = off % chips
         pairs[off].wait_recv()
@@ -261,6 +289,39 @@
     def _():
         for i in peers:
             stage4(i).start()
+
+    value = t2_send[...]
+    for i in (1, 2, 0):
+        top2[i].wait_recv()
+        value = value + t2_recv[i]
+    t_piece = top_ref.at[pl.ds(first_t, rows), mine]
+    t_piece[...] = dielectric(value, t_scale_ref[...], first_t, first_col)
+    top3 = [
+        remote(t_piece, t_piece, t3_s.at[i], t3_r.at[slot], chip(d, core)) for i, (d, core, slot) in enumerate(spread_to)
+    ]
+    for copy in top3:
+        copy.start()
+
+    def quarter(r):
+        return top_ref.at[pl.ds(pl.multiple_of(r * BLOCK, BLOCK), BLOCK), mine]
+
+    def to_column(i):
+        return remote(quarter(gr), quarter(gr), t4_s.at[i - 1], t4_r.at[i - 1], (kb, (gr + i) % grid, gc))
+
+    def to_core(i):
+        r = (gr + grid - i) % grid
+        return remote(quarter(r), quarter(r), t5_s.at[i - 1], t5_r.at[i - 1], partner)
+
+    def send_column():
+        for slot in range(7):
+            remote(t_piece, t_piece, t3_s.at[0], t3_r.at[slot], partner).wait_recv()
+        for i in range(1, grid):
+            to_column(i).start()
+
+    def send_core():
+        for i in range(1, grid):
+            to_column(i).wait_recv()
+            to_core(i).start()
 
     def stage5(i, half):
         r, s = sender(i)
@@ -297,14 +358,9 @@
             far_send_ref[i] = gathered(j, extra)
             far_copy(i).start()
 
-    my_top = top_ref.at[chunk(0), mine]
-
-    def to_top(i):
-        return remote(f_ref, my_top, top_s.at[i - 1], top_r, (kb, (gr + i) % grid, gc))
-
     swap = remote(f_ref.at[pl.ds(pl.multiple_of(other * band, band), band)], own_ref.at[:, mine], swap_s, swap_r, partner)
 
-    def send_top():
+    def send_own():
         value = gathered(0, (8, 10))
         for i in (1, 2, 0):
             far_copy(i).wait_recv()
@@ -312,45 +368,13 @@
         value = dielectric(value, scale_ref[...], first_row, first_col)
         f_ref[...] = value
 
-        @pl.when(is_top)
-        def _():
-            for i in range(1, grid):
-                to_top(i).start()
-            my_top[...] = value
-
         swap.start()
         own_ref[:, mine] = f_ref[pl.ds(pl.multiple_of(c * band, band), band)]
 
-    def piece(off):
-        return top_ref.at[chunk(off), mine]
-
-    def forward(off):
-        return remote(piece(off), piece(off), fw_s.at[off], fw_r.at[off], partner)
-
-    gossip = {
-        0: ((8, 0), (4, 1), (-4, 2), (1, 3), (-1, 4), (2, 5), (-2, 6)),
-        4: ((1, 7), (-1, 8), (-2, 9)),
-        12: ((1, 10), (-1, 11), (2, 12)),
-        8: ((1, 13), (-1, 14)),
-    }
-
-    def gossip_copy(off, delta, i):
-        return remote(piece(off), piece(off), ag_s.at[i], ag_r.at[(off - delta) % chips], chip(delta))
-
-    def arrive(off):
-        remote(piece(off), piece(off), ag_s.at[0], ag_r.at[off], partner).wait_recv()
-
     def to_side(i):
         return remote(own_ref, left_ref, side_s.at[i - 1], side_r, (kb, gr, (gc + i) % grid))
 
-    def send_first():
-        @pl.when(jnp.logical_not(is_top))
-        def _():
-            to_top(1).wait_recv()
-
-        for delta, i in gossip[0]:
-            gossip_copy(0, delta, i).start()
-        forward(0).start()
+    def send_side():
         swap.wait_recv()
 
         @pl.when(is_left)
@@ -358,25 +382,33 @@
             for i in range(1, grid):
                 to_side(i).start()
 
-    def send_second():
-        for off in (4, 12, 8):
-            arrive(off)
-            for delta, i in gossip[off]:
-                gossip_copy(off, delta, i).start()
-            forward(off).start()
-
-    send_far()
-    for i in peers:
-        @pl.when(needed(sender(i)[0], c))
-        def _():
-            stage4(i).wait_recv()
-            stage5(i, mine).start()
-    for i in peers:
-        @pl.when(needed(sender(i)[0], other))
-        def _():
-            stage5(i, theirs).wait_recv()
-
-    plan = {(0, 6): send_top, (0, 15): end_e00_copies, (1, 2): send_first, (3, 0): send_second}
+    def wait_rows(r):
+        for i in peers:
+            @pl.when((sender(i)[0] == r) & needed(r, c))
+            def _():
+                stage4(i).wait_recv()
+                stage5(i, mine).start()
+
+    def wait_halves(r):
+        for i in peers:
+            @pl.when((sender(i)[0] == r) & needed(r, other))
+            def _():
+                stage5(i, theirs).wait_recv()
+
+    def wait_later_rows():
+        for r in range(1, grid):
+            wait_rows(r)
+
+    def wait_later_halves():
+        for r in range(1, grid):
+            wait_halves(r)
+
+    wait_rows(0)
+    wait_halves(0)
+    plan = {
+        (0, 4): wait_later_rows, (0, 8): send_column, (0, 11): wait_later_halves, (0, 13): send_far, (0, 15): end_e00_copies,
+        (2, 8): send_own, (3, 0): send_core, (3, 6): send_side,
+    }
     cuts = [slice(b * BLOCK, (b + 1) * BLOCK) for b in range(width // BLOCK)]
     for b, cut in enumerate(cuts):
         def hook(g):
@@ -413,11 +445,8 @@
     for cut in cuts:
         w_ref[:, cut] = product(low_ref[:, cut.start:], g_ref[cut.start:, cut])
 
-    for off in (1, 15, 2, 14, 5, 3, 13, 11, 6, 10, 7, 9):
-        arrive(off)
-        forward(off).start()
-    for off in range(chips):
-        forward(off).wait_recv()
+    for i in range(1, grid):
+        to_core(i).wait_recv()
 
     row = kb * band + lax.broadcasted_iota(jnp.int32, (band, width), 0)
     col = lax.broadcasted_iota(jnp.int32, (band, width), 1)
@@ -425,20 +454,13 @@
     trail = own_ref[...] - product(w_ref[...], top_ref[...])
     out_ref[...] = jnp.where(is_left, factor_side, jnp.where(is_top, own_ref[...], trail))
 
-    for copy in stage1 + stage2 + list(pairs.values()) + list(near_copies.values()) + [swap]:
+    for copy in stage1 + stage2 + top1 + top2 + top3 + list(pairs.values()) + list(near_copies.values()) + [swap]:
         copy.wait_send()
     for i in range(3):
         far_copy(i).wait_send()
-    for off, sends in gossip.items():
-        for delta, i in sends:
-            gossip_copy(off, delta, i).wait_send()
-    for off in range(chips):
-        forward(off).wait_send()
-
-    @pl.when(is_top)
-    def _():
-        for i in range(1, grid):
-            to_top(i).wait_send()
+    for i in range(1, grid):
+        to_column(i).wait_send()
+        to_core(i).wait_send()
 
     @pl.when(is_left)
     def _():
@@ -476,6 +498,11 @@
             pltpu.VMEM((width, width), f32),
             pltpu.VMEM((owners, width), f32),
             pltpu.VMEM((owners, width), f32),
+            pltpu.VMEM((BLOCK, width), f32),
+            pltpu.VMEM((7,) + piece, f32),
+            pltpu.VMEM(piece, f32),
+            pltpu.VMEM((3,) + piece, f32),
+            pltpu.VMEM(piece, f32),
             pltpu.VMEM((owners * bands, 3 * width), jnp.bfloat16),
             pltpu.VMEM((bands * (total_g // LOW), LOW), jnp.bfloat16),
             pltpu.VMEM((BLOCK, width), f32),
@@ -505,9 +532,11 @@
             dma((3,)), dma((3,)),
             dma, dma,
             dma((grid - 1,)), dma,
-            dma((grid - 1,)), dma,
-            dma((15,)), dma((chips,)),
-            dma((chips,)), dma((chips,)),
+            dma((7,)), dma((7,)),
+            dma((3,)), dma((3,)),
+            dma((7,)), dma((7,)),
+            dma((grid - 1,)), dma((grid - 1,)),
+            dma((grid - 1,)), dma((grid - 1,)),
             dma((5,)),
         ],
         compiler_params=pltpu.CompilerParams(

time: 70.8 us -> 70 us (0.989)
  the two profiles are of different devices: /device:TPU:1 before, /device:TPU:89 now
where the time goes in v3:
time: 70 us; the launch traced here: 69.8 us
  Pallas kernels  67.7 us (97%)
  local copies, waits for them, and re-layouts  1.38 us (2%)
    pallas_call x1, Pallas kernels, body(): pl.pallas_call(functools.partial(whole_kernel, chips, grid), out_shape=ja...  67.7 us

profile of v3, /device:TPU:89, one launch (start us, length us, event | category | flops | bytes accessed | tf_op | source)
XLA Modules:
  0.0 69.8 jit_solution(254660628667246380)
XLA Ops:
  0.7 67.7 %whole.1 = f32[16,512]{1,0:T(8,128)} custom-call(s32[17,32]{1,0:T(8,128)} %bitcast.5, s32[17,32]{1,0:T(8,128)} %bitcast.6, bf16[16,2048]{1,0:T(8,128)(2,1)} %bitcast.4, f32[1,1]{1,0:T(1,128)S(6)} %copy.9.ec_ref, f32[1,16]{1,0:T(1,128)} %ev_ref.1, f32[1,2048]{1,0:T(1,128)} %bitcast.7, s32[48,2048]{1,0:T(8,128)} %gmap_hbm.1), custom_call_target="tpu_custom_call" | custom-call | tf_op jit(solution)/shard_map/whole/pallas_call | solution.py:486
  68.4 1.4 %copy.10 = f32[16,512]{1,0:T(8,128)} copy(f32[16,512]{1,0:T(8,128)} %whole.1) | data formatting | bytes 65536

commit v4 on v3

--- a/solution.py
+++ b/solution.py
@@ -18,22 +18,39 @@
     return lax.dot_general(a, b, dims, precision=HI, preferred_element_type=jnp.float32)
 
 
+def thirds(a):
+    first = a.astype(jnp.bfloat16).astype(jnp.float32)
+    second = (a - first).astype(jnp.bfloat16).astype(jnp.float32)
+    return first, second, a - first - second
+
+
+def gram(rows):
+    p, q, r = thirds(rows)
+    one = jnp.concatenate([p, p, q, p, r, q], axis=0).astype(jnp.bfloat16)
+    two = jnp.concatenate([p, q, p, r, p, q], axis=0).astype(jnp.bfloat16)
+    return lax.dot_general(one, two, TN, preferred_element_type=jnp.float32)
+
+
 def inverse_factor(d, hook):
     n = d.shape[0]
+    groups = n // 8
     lane = lax.broadcasted_iota(jnp.int32, (8, n), 1)
     sub = lax.broadcasted_iota(jnp.int32, (8, n), 0)
-    tail = d.reshape(n // 8, 8, n)
+    rows = [d[8 * i:8 * i + 8, :] for i in range(groups)]
     out = []
-    for g in range(n // 8):
+    for g in range(groups):
         base = 8 * g
         hook(g)
-        cols = [jnp.broadcast_to(tail[:, :, base + k:base + k + 1], tail.shape) for k in range(8)]
+        follows = g + 1 < groups
+        head, after = rows[g], rows[g + 1] if follows else None
+        cols = [jnp.broadcast_to(head[:, base + k:base + k + 1], (8, n)) for k in range(8)]
+        below = [jnp.broadcast_to(after[:, base + k:base + k + 1], (8, n)) for k in range(8)] if follows else None
         inside = (lane >= base) & (lane < base + 8)
-        head = jnp.where(inside, jnp.where(lane - base == sub, 1.0, 0.0), tail[0])
-        rest = jnp.where(inside[None], 0.0, tail[1:]) if g + 1 < n // 8 else None
-        entry = {(i, k): jnp.broadcast_to(cols[k][0, i:i + 1, :], (8, n)) for i in range(8) for k in range(i + 1)}
+        head = jnp.where(inside, jnp.where(lane - base == sub, 1.0, 0.0), head)
+        if follows:
+            after = jnp.where(inside, 0.0, after)
+        entry = {(i, k): jnp.broadcast_to(cols[k][i:i + 1, :], (8, n)) for i in range(8) for k in range(i + 1)}
         row = [jnp.broadcast_to(head[i:i + 1, :], (8, n)) for i in range(8)]
-        below = [c[1:] for c in cols]
         done = jnp.zeros((8, n), jnp.float32)
         for j in range(8):
             scale = lax.rsqrt(entry[j, j])
@@ -44,13 +61,18 @@
                 row[i] = row[i] - mult[i] * pivot_row
                 for k in range(j + 1, i + 1):
                     entry[i, k] = entry[i, k] - mult[i] * mult[k]
-            if rest is not None:
-                step = below[j] * scale[None]
-                rest = rest - step * pivot_row[None]
+            if follows:
+                step = below[j] * scale
+                after = after - step * pivot_row
                 for k in range(j + 1, 8):
-                    below[k] = below[k] - step * mult[k][None]
+                    below[k] = below[k] - step * mult[k]
         out.append(jnp.where(lane <= sub + base, done, 0.0))
-        tail = rest
+        if follows:
+            rows[g + 1] = after
+        if g + 2 < groups:
+            change = gram(done)
+            for i in range(g + 2, groups):
+                rows[i] = jnp.where(inside, 0.0, rows[i]) - change[8 * i:8 * i + 8, :]
     return jnp.concatenate(out, axis=0)
 
 

time: 70 us -> 69.5 us (level)
  the two profiles are of different devices: /device:TPU:89 before, /device:TPU:92 now
where the time goes in v4:
time: 69.5 us; the launch traced here: 69.3 us
  Pallas kernels  67.3 us (97%)
  local copies, waits for them, and re-layouts  1.38 us (2%)
    pallas_call x1, Pallas kernels, body(): pl.pallas_call(functools.partial(whole_kernel, chips, grid), out_shape=ja...  67.3 us

profile of v4, /device:TPU:92, one launch (start us, length us, event | category | flops | bytes accessed | tf_op | source)
XLA Modules:
  0.0 69.3 jit_solution(9909170554664703209)
XLA Ops:
  0.7 67.3 %whole.1 = f32[16,512]{1,0:T(8,128)} custom-call(s32[17,32]{1,0:T(8,128)} %bitcast.5, s32[17,32]{1,0:T(8,128)} %bitcast.6, bf16[16,2048]{1,0:T(8,128)(2,1)} %bitcast.4, f32[1,1]{1,0:T(1,128)S(6)} %copy.9.ec_ref, f32[1,16]{1,0:T(1,128)} %ev_ref.1, f32[1,2048]{1,0:T(1,128)} %bitcast.7, s32[48,2048]{1,0:T(8,128)} %gmap_hbm.1), custom_call_target="tpu_custom_call" | custom-call | tf_op jit(solution)/shard_map/whole/pallas_call | solution.py:508
  68.0 1.4 %copy.10 = f32[16,512]{1,0:T(8,128)} copy(f32[16,512]{1,0:T(8,128)} %whole.1) | data formatting | bytes 65536

commit v5 on v4

--- a/solution.py
+++ b/solution.py
@@ -52,20 +52,26 @@
         entry = {(i, k): jnp.broadcast_to(cols[k][i:i + 1, :], (8, n)) for i in range(8) for k in range(i + 1)}
         row = [jnp.broadcast_to(head[i:i + 1, :], (8, n)) for i in range(8)]
         done = jnp.zeros((8, n), jnp.float32)
-        for j in range(8):
-            scale = lax.rsqrt(entry[j, j])
+        for j in range(0, 8, 2):
+            a, b, d2 = entry[j, j], entry[j + 1, j], entry[j + 1, j + 1]
+            scale = lax.rsqrt(a)
+            cross = b * scale
+            scale2 = lax.rsqrt(a * d2 - b * b) * (a * scale)
             pivot_row = row[j] * scale
-            done = jnp.where(sub == j, pivot_row, done)
-            mult = {i: entry[i, j] * scale for i in range(j + 1, 8)}
-            for i in range(j + 1, 8):
-                row[i] = row[i] - mult[i] * pivot_row
-                for k in range(j + 1, i + 1):
-                    entry[i, k] = entry[i, k] - mult[i] * mult[k]
+            pivot_row2 = (row[j + 1] - cross * pivot_row) * scale2
+            done = jnp.where(sub == j, pivot_row, jnp.where(sub == j + 1, pivot_row2, done))
+            mult = {i: entry[i, j] * scale for i in range(j + 2, 8)}
+            mult2 = {i: (entry[i, j + 1] - cross * mult[i]) * scale2 for i in range(j + 2, 8)}
+            for i in range(j + 2, 8):
+                row[i] = (row[i] - mult[i] * pivot_row) - mult2[i] * pivot_row2
+                for k in range(j + 2, i + 1):
+                    entry[i, k] = (entry[i, k] - mult[i] * mult[k]) - mult2[i] * mult2[k]
             if follows:
                 step = below[j] * scale
-                after = after - step * pivot_row
-                for k in range(j + 1, 8):
-                    below[k] = below[k] - step * mult[k]
+                step2 = (below[j + 1] - step * cross) * scale2
+                after = (after - step * pivot_row) - step2 * pivot_row2
+                for k in range(j + 2, 8):
+                    below[k] = (below[k] - step * mult[k]) - step2 * mult2[k]
         out.append(jnp.where(lane <= sub + base, done, 0.0))
         if follows:
             rows[g + 1] = after
@@ -285,6 +291,26 @@
         pairs[off].wait_recv()
         return total_ref[chunk(off), mine] + pair_ref[order.index(off)]
 
+    for slot in range(7):
+        remote(part, part, c3_s.at[0], c3_r.at[slot], partner).wait_recv()
+
+    def e00_part(r, s, half):
+        return e00_ref.at[pl.ds(pl.multiple_of(r * BLOCK + s * rows, rows), rows), half]
+
+    def needed(r, core):
+        return jnp.logical_or(core == 1, r < 2)
+
+    def stage4(i):
+        return remote(e00_part(gr, gc, mine), e00_part(gr, gc, mine), c4_s.at[i], c4_r.at[i], peers[i])
+
+    def sender(i):
+        return (gr + grid - i // grid) % grid, (gc + grid - i % grid) % grid
+
+    @pl.when(needed(gr, c))
+    def _():
+        for i in peers:
+            stage4(i).start()
+
     near_copies = {}
     for off, delta, slot in near:
         send_ref[slot] = own_part(off)
@@ -292,37 +318,19 @@
         copy.start()
         near_copies[slot] = copy
 
-    for slot in range(7):
-        remote(part, part, c3_s.at[0], c3_r.at[slot], partner).wait_recv()
-
-    def e00_part(r, s, half):
-        return e00_ref.at[pl.ds(pl.multiple_of(r * BLOCK + s * rows, rows), rows), half]
-
-    def needed(r, core):
-        return jnp.logical_or(core == 1, r < 2)
-
-    def stage4(i):
-        return remote(e00_part(gr, gc, mine), e00_part(gr, gc, mine), c4_s.at[i], c4_r.at[i], peers[i])
-
-    def sender(i):
-        return (gr + grid - i // grid) % grid, (gc + grid - i % grid) % grid
-
-    @pl.when(needed(gr, c))
-    def _():
-        for i in peers:
-            stage4(i).start()
-
-    value = t2_send[...]
-    for i in (1, 2, 0):
-        top2[i].wait_recv()
-        value = value + t2_recv[i]
     t_piece = top_ref.at[pl.ds(first_t, rows), mine]
-    t_piece[...] = dielectric(value, t_scale_ref[...], first_t, first_col)
     top3 = [
         remote(t_piece, t_piece, t3_s.at[i], t3_r.at[slot], chip(d, core)) for i, (d, core, slot) in enumerate(spread_to)
     ]
-    for copy in top3:
-        copy.start()
+
+    def send_pieces():
+        value = t2_send[...]
+        for i in (1, 2, 0):
+            top2[i].wait_recv()
+            value = value + t2_recv[i]
+        t_piece[...] = dielectric(value, t_scale_ref[...], first_t, first_col)
+        for copy in top3:
+            copy.start()
 
     def quarter(r):
         return top_ref.at[pl.ds(pl.multiple_of(r * BLOCK, BLOCK), BLOCK), mine]
@@ -428,8 +436,8 @@
     wait_rows(0)
     wait_halves(0)
     plan = {
-        (0, 4): wait_later_rows, (0, 8): send_column, (0, 11): wait_later_halves, (0, 13): send_far, (0, 15): end_e00_copies,
-        (2, 8): send_own, (3, 0): send_core, (3, 6): send_side,
+        (0, 2): send_pieces, (0, 6): wait_later_rows, (0, 11): wait_later_halves, (0, 15): end_e00_copies,
+        (1, 0): send_far, (1, 2): send_column, (2, 15): send_own, (3, 1): send_core, (3, 7): send_side,
     }
     cuts = [slice(b * BLOCK, (b + 1) * BLOCK) for b in range(width // BLOCK)]
     for b, cut in enumerate(cuts):

time: 69.5 us -> 70.1 us (level)
  the two profiles are of different devices: /device:TPU:92 before, /device:TPU:1 now
where the time goes in v5:
time: 70.1 us; the launch traced here: 69.8 us
  Pallas kernels  67.8 us (97%)
  local copies, waits for them, and re-layouts  1.38 us (2%)
    pallas_call x1, Pallas kernels, body(): pl.pallas_call(functools.partial(whole_kernel, chips, grid), out_shape=ja...  67.8 us

profile of v5, /device:TPU:1, one launch (start us, length us, event | category | flops | bytes accessed | tf_op | source)
XLA Modules:
  0.0 69.8 jit_solution(2929470362165994834)
XLA Ops:
  0.7 67.8 %whole.1 = f32[16,512]{1,0:T(8,128)} custom-call(s32[17,32]{1,0:T(8,128)} %bitcast.5, s32[17,32]{1,0:T(8,128)} %bitcast.6, bf16[16,2048]{1,0:T(8,128)(2,1)} %bitcast.4, f32[1,1]{1,0:T(1,128)S(6)} %copy.9.ec_ref, f32[1,16]{1,0:T(1,128)} %ev_ref.1, f32[1,2048]{1,0:T(1,128)} %bitcast.7, s32[48,2048]{1,0:T(8,128)} %gmap_hbm.1), custom_call_target="tpu_custom_call" | custom-call | tf_op jit(solution)/shard_map/whole/pallas_call | solution.py:516
  68.5 1.4 %copy.10 = f32[16,512]{1,0:T(8,128)} copy(f32[16,512]{1,0:T(8,128)} %whole.1) | data formatting | bytes 65536

commit v6 on v5

--- a/solution.py
+++ b/solution.py
@@ -87,7 +87,7 @@
                  lo_ref, hi_ref, pt_ref, t1_recv, t2_send, t2_recv, t_scale_ref, s_ref, y_ref, p_ref, c1_recv, c2_send, c2_recv, e00_ref, total_ref,
                  pair_ref, send_ref, recv_ref, far_send_ref, far_recv_ref, f_ref, own_ref, left_ref, top_ref,
                  low_ref, w_ref,
-                 c1_s, c1_r, c2_s, c2_r, c3_s, c3_r, c4_s, c4_r, c5_s, c5_r,
+                 c1_s, c1_r, c2_s, c2_r, c3_s, c3_r, c4_s, c4_r, c5_s, c5_r, c6_s, c6_r, c7_s, c7_r,
                  pair_s, pair_r, near_s, near_r, far_s, far_r, swap_s, swap_r,
                  side_s, side_r, t1_s, t1_r, t2_s, t2_r, t3_s, t3_r, t4_s, t4_r, t5_s, t5_r, in_s):
     kb, gr, gc = lax.axis_index("kb"), lax.axis_index("gr"), lax.axis_index("gc")
@@ -297,26 +297,35 @@
     def e00_part(r, s, half):
         return e00_ref.at[pl.ds(pl.multiple_of(r * BLOCK + s * rows, rows), rows), half]
 
-    def needed(r, core):
-        return jnp.logical_or(core == 1, r < 2)
-
-    def stage4(i):
-        return remote(e00_part(gr, gc, mine), e00_part(gr, gc, mine), c4_s.at[i], c4_r.at[i], peers[i])
+    def whole_half(r, core):
+        return jnp.logical_or(core == 1, r == 1)
+
+    def cut_half(r, core):
+        return jnp.logical_and(core == 0, r == 0)
+
+    tile, rest = slice(0, BLOCK), slice(BLOCK, wide)
+
+    def stage4(i, half, sends=None, recvs=None):
+        part = e00_part(gr, gc, half)
+        return remote(part, part, (c4_s if sends is None else sends).at[i], (c4_r if recvs is None else recvs).at[i], peers[i])
+
+    def stage4_tile(i):
+        return stage4(i, tile, c6_s, c6_r)
 
     def sender(i):
         return (gr + grid - i // grid) % grid, (gc + grid - i % grid) % grid
 
-    @pl.when(needed(gr, c))
+    @pl.when(cut_half(gr, c))
     def _():
         for i in peers:
-            stage4(i).start()
-
-    near_copies = {}
-    for off, delta, slot in near:
-        send_ref[slot] = own_part(off)
-        copy = remote(send_ref.at[slot], recv_ref.at[slot], near_s.at[slot], near_r.at[slot], chip(delta))
-        copy.start()
-        near_copies[slot] = copy
+            stage4_tile(i).start()
+        for i in peers:
+            stage4(i, rest).start()
+
+    @pl.when(whole_half(gr, c))
+    def _():
+        for i in peers:
+            stage4(i, mine).start()
 
     t_piece = top_ref.at[pl.ds(first_t, rows), mine]
     top3 = [
@@ -357,6 +366,10 @@
         r, s = sender(i)
         return remote(e00_part(r, s, half), e00_part(r, s, half), c5_s.at[i], c5_r.at[i], partner)
 
+    def stage5_tile(i):
+        r, s = sender(i)
+        return remote(e00_part(r, s, tile), e00_part(r, s, tile), c7_s.at[i], c7_r.at[i], partner)
+
 
     def gathered(j, extra):
         value = own_part(4 * j)
@@ -374,12 +387,23 @@
         for copy in stage3:
             copy.wait_send()
 
-        @pl.when(needed(gr, c))
+        @pl.when(cut_half(gr, c))
         def _():
             for i in peers:
-                stage4(i).wait_send()
-        for i in peers:
-            @pl.when(needed(sender(i)[0], c))
+                stage4_tile(i).wait_send()
+                stage4(i, rest).wait_send()
+
+        @pl.when(whole_half(gr, c))
+        def _():
+            for i in peers:
+                stage4(i, mine).wait_send()
+        for i in peers:
+            @pl.when(cut_half(sender(i)[0], c))
+            def _():
+                stage5_tile(i).wait_send()
+                stage5(i, rest).wait_send()
+
+            @pl.when(whole_half(sender(i)[0], c))
             def _():
                 stage5(i, mine).wait_send()
 
@@ -412,31 +436,52 @@
             for i in range(1, grid):
                 to_side(i).start()
 
-    def wait_rows(r):
-        for i in peers:
-            @pl.when((sender(i)[0] == r) & needed(r, c))
-            def _():
-                stage4(i).wait_recv()
+    def wait_rows():
+        for i in peers:
+            @pl.when(cut_half(sender(i)[0], c))
+            def _():
+                stage4(i, rest).wait_recv()
+                stage5(i, rest).start()
+
+            @pl.when(whole_half(sender(i)[0], c))
+            def _():
+                stage4(i, mine).wait_recv()
                 stage5(i, mine).start()
 
-    def wait_halves(r):
-        for i in peers:
-            @pl.when((sender(i)[0] == r) & needed(r, other))
+    def wait_halves():
+        for i in peers:
+            @pl.when(cut_half(sender(i)[0], other))
+            def _():
+                stage5(i, rest).wait_recv()
+
+            @pl.when(whole_half(sender(i)[0], other))
             def _():
                 stage5(i, theirs).wait_recv()
 
-    def wait_later_rows():
-        for r in range(1, grid):
-            wait_rows(r)
-
-    def wait_later_halves():
-        for r in range(1, grid):
-            wait_halves(r)
-
-    wait_rows(0)
-    wait_halves(0)
+    near_copies = {}
+    for off, delta, slot in near:
+        send_ref[slot] = own_part(off)
+        copy = remote(send_ref.at[slot], recv_ref.at[slot], near_s.at[slot], near_r.at[slot], chip(delta))
+        copy.start()
+        near_copies[slot] = copy
+
+    @pl.when(c == 0)
+    def _():
+        for i in peers:
+            @pl.when(sender(i)[0] == 0)
+            def _():
+                stage4_tile(i).wait_recv()
+                stage5_tile(i).start()
+
+    @pl.when(c == 1)
+    def _():
+        for i in peers:
+            @pl.when(sender(i)[0] == 0)
+            def _():
+                stage5_tile(i).wait_recv()
+
     plan = {
-        (0, 2): send_pieces, (0, 6): wait_later_rows, (0, 11): wait_later_halves, (0, 15): end_e00_copies,
+        (0, 2): send_pieces, (0, 5): wait_rows, (0, 11): wait_halves, (0, 15): end_e00_copies,
         (1, 0): send_far, (1, 2): send_column, (2, 15): send_own, (3, 1): send_core, (3, 7): send_side,
     }
     cuts = [slice(b * BLOCK, (b + 1) * BLOCK) for b in range(width // BLOCK)]
@@ -557,6 +602,8 @@
             dma((7,)), dma((7,)),
             dma((grid * grid,)), dma((grid * grid,)),
             dma((grid * grid,)), dma((grid * grid,)),
+            dma((grid * grid,)), dma((grid * grid,)),
+            dma((grid * grid,)), dma((grid * grid,)),
             dma((chips,)), dma((chips,)),
             dma((12,)), dma((12,)),
             dma((3,)), dma((3,)),

time: 70.1 us -> 68.2 us (0.973)
  Pallas kernels: 67.8 us -> 65.3 us
    pallas_call x1, Pallas kernels: 67.8 us -> 65.3 us  [body(): pl.pallas_call(functools.partial(whole_kernel, chips, grid), out_shape=ja...]
where the time goes in v6:
time: 68.2 us; the launch traced here: 67.3 us
  Pallas kernels  65.3 us (96%)
  local copies, waits for them, and re-layouts  1.38 us (2%)
    pallas_call x1, Pallas kernels, body(): pl.pallas_call(functools.partial(whole_kernel, chips, grid), out_shape=ja...  65.3 us
    unnamed x1, local copies, waits for them, and re-layouts  1.38 us

profile of v6, /device:TPU:1, one launch (start us, length us, event | category | flops | bytes accessed | tf_op | source)
XLA Modules:
  0.0 67.3 jit_solution(9797718199496274919)
XLA Ops:
  0.7 65.3 %whole.1 = f32[16,512]{1,0:T(8,128)} custom-call(s32[17,32]{1,0:T(8,128)} %bitcast.5, s32[17,32]{1,0:T(8,128)} %bitcast.6, bf16[16,2048]{1,0:T(8,128)(2,1)} %bitcast.4, f32[1,1]{1,0:T(1,128)S(6)} %copy.9.ec_ref, f32[1,16]{1,0:T(1,128)} %ev_ref.1, f32[1,2048]{1,0:T(1,128)} %bitcast.7, s32[48,2048]{1,0:T(8,128)} %gmap_hbm.1), custom_call_target="tpu_custom_call" | custom-call | tf_op jit(solution)/shard_map/whole/pallas_call | solution.py:561
  65.9 1.4 %copy.10 = f32[16,512]{1,0:T(8,128)} copy(f32[16,512]{1,0:T(8,128)} %whole.1) | data formatting | bytes 65536

commit v7 on v6

--- a/solution.py
+++ b/solution.py
@@ -208,28 +208,6 @@
     theirs = pl.ds(pl.multiple_of(other * wide, wide), wide)
 
     gather(2, pl.multiple_of(gc * width, width))
-    pt_ref[...] = lax.dot_general(
-        s_ref[:, pl.ds(pl.multiple_of(gr * BLOCK, BLOCK), BLOCK)], s_ref[:, 2 * width:], TN, preferred_element_type=jnp.float32
-    )
-
-    def t_part(delta, core):
-        k = (z + delta + chips) % grid
-        return pt_ref.at[pl.ds(pl.multiple_of(rows * k, rows), rows), pl.ds(pl.multiple_of(core * wide, wide), wide)]
-
-    top1 = [
-        remote(t_part(d, core), t1_recv.at[slot], t1_s.at[i], t1_r.at[slot], chip(d, core))
-        for i, (d, core, slot) in enumerate(near_parts)
-    ]
-    for copy in top1:
-        copy.start()
-
-    first_e = pl.multiple_of(gr * BLOCK + gc * rows + 8 * (z % grid), 8)
-    scale_e = scale_of(first_e, c * wide, 8, wide)
-    first_row, first_col = gr * width + z * rows, gc * width + c * wide
-    first_t = pl.multiple_of(gr * BLOCK + rows * (z % grid), rows)
-    scale_ref[...] = scale_of(first_row, first_col, rows, wide)
-    t_scale_ref[...] = scale_of(first_t, first_col, rows, wide)
-
     value = p_part(0, c)[...]
     for slot in range(7):
         remote(p_part(0, other), c1_recv.at[slot], c1_s.at[0], c1_r.at[slot], partner).wait_recv()
@@ -241,26 +219,29 @@
     for copy in stage2:
         copy.start()
 
+    pt_ref[...] = lax.dot_general(
+        s_ref[:, pl.ds(pl.multiple_of(gr * BLOCK, BLOCK), BLOCK)], s_ref[:, 2 * width:], TN, preferred_element_type=jnp.float32
+    )
+
+    def t_part(delta, core):
+        k = (z + delta + chips) % grid
+        return pt_ref.at[pl.ds(pl.multiple_of(rows * k, rows), rows), pl.ds(pl.multiple_of(core * wide, wide), wide)]
+
+    top1 = [
+        remote(t_part(d, core), t1_recv.at[slot], t1_s.at[i], t1_r.at[slot], chip(d, core))
+        for i, (d, core, slot) in enumerate(near_parts)
+    ]
+    for copy in top1:
+        copy.start()
+
+    first_e = pl.multiple_of(gr * BLOCK + gc * rows + 8 * (z % grid), 8)
+    scale_e = scale_of(first_e, c * wide, 8, wide)
+    first_row, first_col = gr * width + z * rows, gc * width + c * wide
+    first_t = pl.multiple_of(gr * BLOCK + rows * (z % grid), rows)
+    scale_ref[...] = scale_of(first_row, first_col, rows, wide)
+    t_scale_ref[...] = scale_of(first_t, first_col, rows, wide)
+
     gather(1, pl.multiple_of(gr * width, width))
-    total_ref[...] = lax.dot_general(
-        s_ref[:, width:2 * width], s_ref[:, 2 * width:], TN, preferred_element_type=jnp.float32
-    )
-
-    def chunk(off):
-        return pl.ds(pl.multiple_of(((z + off + chips) % chips) * rows, rows), rows)
-
-    near = [
-        (9, 1, 2), (7, -1, 6), (5, 1, 1), (3, -1, 5), (6, 2, 9), (-6, -2, 11),
-        (13, 1, 3), (11, -1, 7), (1, 1, 0), (15, -1, 4), (2, 2, 8), (-2, -2, 10),
-    ]
-    order = [off % chips for off, _, _ in near] + [8, 4, 12, 0]
-    pairs = {
-        off: remote(total_ref.at[chunk(off), theirs], pair_ref.at[i], pair_s.at[i], pair_r.at[i], partner)
-        for i, off in enumerate(order)
-    }
-    for off in order:
-        pairs[off].start()
-
     value = c2_send[...]
     for i in (1, 2, 0):
         stage2[i].wait_recv()
@@ -285,6 +266,25 @@
     ]
     for copy in top2:
         copy.start()
+
+    total_ref[...] = lax.dot_general(
+        s_ref[:, width:2 * width], s_ref[:, 2 * width:], TN, preferred_element_type=jnp.float32
+    )
+
+    def chunk(off):
+        return pl.ds(pl.multiple_of(((z + off + chips) % chips) * rows, rows), rows)
+
+    near = [
+        (9, 1, 2), (7, -1, 6), (5, 1, 1), (3, -1, 5), (6, 2, 9), (-6, -2, 11),
+        (13, 1, 3), (11, -1, 7), (1, 1, 0), (15, -1, 4), (2, 2, 8), (-2, -2, 10),
+    ]
+    order = [off % chips for off, _, _ in near] + [8, 4, 12, 0]
+    pairs = {
+        off: remote(total_ref.at[chunk(off), theirs], pair_ref.at[i], pair_s.at[i], pair_r.at[i], partner)
+        for i, off in enumerate(order)
+    }
+    for off in order:
+        pairs[off].start()
 
     def own_part(off):
         off = off % chips

time: 68.2 us -> 68.1 us (level); the launches traced: 67.3 us -> 67.9 us
  no operation moved by 1% of the time
where the time goes in v7:
time: 68.1 us; the launch traced here: 67.9 us
  Pallas kernels  65.9 us (97%)
  local copies, waits for them, and re-layouts  1.38 us (2%)
    pallas_call x1, Pallas kernels, body(): pl.pallas_call(functools.partial(whole_kernel, chips, grid), out_shape=ja...  65.9 us
    unnamed x1, local copies, waits for them, and re-layouts  1.38 us

profile of v7, /device:TPU:1, one launch (start us, length us, event | category | flops | bytes accessed | tf_op | source)
XLA Modules:
  0.0 67.9 jit_solution(18173427651063955127)
XLA Ops:
  0.7 65.9 %whole.1 = f32[16,512]{1,0:T(8,128)} custom-call(s32[17,32]{1,0:T(8,128)} %bitcast.5, s32[17,32]{1,0:T(8,128)} %bitcast.6, bf16[16,2048]{1,0:T(8,128)(2,1)} %bitcast.4, f32[1,1]{1,0:T(1,128)S(6)} %copy.9.ec_ref, f32[1,16]{1,0:T(1,128)} %ev_ref.1, f32[1,2048]{1,0:T(1,128)} %bitcast.7, s32[48,2048]{1,0:T(8,128)} %gmap_hbm.1), custom_call_target="tpu_custom_call" | custom-call | tf_op jit(solution)/shard_map/whole/pallas_call | solution.py:561
  66.6 1.4 %copy.10 = f32[16,512]{1,0:T(8,128)} copy(f32[16,512]{1,0:T(8,128)} %whole.1) | data formatting | bytes 65536

commit v8 on v7

--- a/solution.py
+++ b/solution.py
@@ -167,7 +167,7 @@
             s_ref[pl.ds(pl.multiple_of(o * bands, bands), bands), side * width:(side + 1) * width] = picked.astype(jnp.bfloat16)
             return carry
 
-        lax.fori_loop(0, owners, pick, 0, unroll=4)
+        lax.fori_loop(0, owners, pick, 0, unroll=16)
 
     root = jnp.sqrt(coulomb_ref[...])
 

time: 68.1 us -> 68.1 us (level)
  no operation moved by 1% of the time
where the time goes in v8:
time: 68.1 us; the launch traced here: 67.9 us
  Pallas kernels  65.8 us (97%)
  local copies, waits for them, and re-layouts  1.38 us (2%)
    pallas_call x1, Pallas kernels, body(): pl.pallas_call(functools.partial(whole_kernel, chips, grid), out_shape=ja...  65.8 us
    unnamed x1, local copies, waits for them, and re-layouts  1.38 us

profile of v8, /device:TPU:1, one launch (start us, length us, event | category | flops | bytes accessed | tf_op | source)
XLA Modules:
  0.0 67.9 jit_solution(7761338943837651318)
XLA Ops:
  0.7 65.8 %whole.1 = f32[16,512]{1,0:T(8,128)} custom-call(s32[17,32]{1,0:T(8,128)} %bitcast.5, s32[17,32]{1,0:T(8,128)} %bitcast.6, bf16[16,2048]{1,0:T(8,128)(2,1)} %bitcast.4, f32[1,1]{1,0:T(1,128)S(6)} %copy.9.ec_ref, f32[1,16]{1,0:T(1,128)} %ev_ref.1, f32[1,2048]{1,0:T(1,128)} %bitcast.7, s32[48,2048]{1,0:T(8,128)} %gmap_hbm.1), custom_call_target="tpu_custom_call" | custom-call | tf_op jit(solution)/shard_map/whole/pallas_call | solution.py:561
  66.5 1.4 %copy.10 = f32[16,512]{1,0:T(8,128)} copy(f32[16,512]{1,0:T(8,128)} %whole.1) | data formatting | bytes 65536
